TPU v7x, 32 devices: a whole 2x2x4 slice. The times are simulated.
32 devices in a mesh: dp: 2 (over core), fsdp: 16 (over z, y, x).
Axes of the slice: x: 2, y: 2, z: 4, core: 2. Of those that a mesh axis runs over, the one named last changes fastest.
Arguments:
- table: bfloat16 [32768, 768], P(('dp', 'fsdp')), may hold values from -6 to 6
- token_ids: int32 [384, 64], P(('dp', 'fsdp')), may hold values from 0 to 32767, as said below
- sent_lengths: int32 [384], P(('dp', 'fsdp')), may hold values from 2 to 64, as said below
- pair_slot: int32 [384], replicated, may hold values from 0 to 383, as said below
- pair_lang: int32 [192], replicated, may hold values from 0 to 108, as said below
- w_query: bfloat16 [768, 768], P('fsdp'), may hold values from -0.21875 to 0.21875
- b_query: bfloat16 [768], P('fsdp'), may hold values from -3 to 3
- w_key: bfloat16 [768, 768], P('fsdp'), may hold values from -0.21875 to 0.21875
- w_value: bfloat16 [768, 768], P('fsdp'), may hold values from -0.21875 to 0.21875
- b_value: bfloat16 [768], P('fsdp'), may hold values from -3 to 3
- w_out: bfloat16 [768, 768], P('fsdp'), may hold values from -1.25 to 1.25
- b_out: bfloat16 [768], P('fsdp'), may hold values from -3 to 3
- ln1_gain: bfloat16 [768], P('fsdp'), may hold values from 0.5 to 1.5
- ln1_bias: bfloat16 [768], P('fsdp'), may hold values from -2 to 2
- w_up: bfloat16 [768, 3072], P('fsdp'), may hold values from -0.21875 to 0.21875
- b_up: bfloat16 [3072], P('fsdp'), may hold values from -3 to 3
- w_down: bfloat16 [3072, 768], P('fsdp'), may hold values from -0.109375 to 0.109375
- b_down: bfloat16 [768], P('fsdp'), may hold values from -3 to 3
- ln2_gain: bfloat16 [768], P('fsdp'), may hold values from 0.5 to 1.5
- ln2_bias: bfloat16 [768], P('fsdp'), may hold values from -2 to 2
Outputs:
- layer_out: bfloat16 [384, 64, 768], P(('dp', 'fsdp'))
- loss_value: float32 [], replicated
- table_grad: float32 [32768, 768], P(('dp', 'fsdp'))
- grad_w_query: float32 [768, 768], P('fsdp')
- grad_b_query: float32 [768], P('fsdp')
- grad_w_key: float32 [768, 768], P('fsdp')
- grad_w_value: float32 [768, 768], P('fsdp')
- grad_b_value: float32 [768], P('fsdp')
- grad_w_out: float32 [768, 768], P('fsdp')
- grad_b_out: float32 [768], P('fsdp')
- grad_ln1_gain: float32 [768], P('fsdp')
- grad_ln1_bias: float32 [768], P('fsdp')
- grad_w_up: float32 [768, 3072], P('fsdp')
- grad_b_up: float32 [3072], P('fsdp')
- grad_w_down: float32 [3072, 768], P('fsdp')
- grad_b_down: float32 [768], P('fsdp')
- grad_ln2_gain: float32 [768], P('fsdp')
- grad_ln2_bias: float32 [768], P('fsdp')
Inputs may be any that keep to these rules, and one draw needn't show every extreme that they name: `token_ids`: among the 768 tokens of one device, at most 48 name rows of any one aligned block of 1024 table rows, and on every device some block is named exactly 48 times. `sent_lengths`: position 0 of a sentence is its summary token; positions at or past its length are padding. Some sentence has length exactly 64. `pair_slot`: each value appears once; slots 2 p and 2 p + 1 are the two sides of translation pair p. `pair_lang`: language pairs have uneven counts of translation pairs.
All inputs are finite; a program needn't handle non-finite values.
Results may differ from a plain program's by a relative error of at most 0.028.
The roundings to bfloat16 on the way count: a program that leaves them out, or rounds other values in their place, can miss the bound.
Values may be sent and summed in bfloat16 or wider, within the bound.
A program may use at most 192 MiB of HBM per device.

v0:
```python
from functools import partial
from types import SimpleNamespace

import jax
import jax.numpy as jnp
from jax import lax
from jax.experimental import pallas as pl
from jax.experimental.pallas import tpu as pltpu
from jax.sharding import PartitionSpec as P

HEADS = 12
HEAD = 64
LANGS = 109


EPSILON = 1e-06
SCORE_SCALE = 50.0
MARGIN_WIDTH = 0.3
MASK_FLOOR = -1000000000.0


def contract(left_side, right_side, left_dim, right_dim):
    return lax.dot_general(
        left_side,
        right_side,
        (((left_dim,), (right_dim,)), ((), ())),
        preferred_element_type=jnp.float32,
    )


def norm_rows(inputs, ln_gain, ln_shift):
    row_mean = jnp.mean(inputs, axis=-1, keepdims=True)
    centered = inputs - row_mean
    variance = jnp.mean(centered * centered, axis=-1, keepdims=True)
    inverse = lax.rsqrt(variance + EPSILON)
    normed = centered * inverse
    return (normed * ln_gain + ln_shift, normed, inverse)


def norm_back(grad_output, normed, inverse, ln_gain):
    grad_normed = grad_output * ln_gain
    first_term = jnp.mean(grad_normed, axis=-1, keepdims=True)
    second_term = jnp.mean(grad_normed * normed, axis=-1, keepdims=True)
    grad_input = inverse * (grad_normed - first_term - normed * second_term)
    return (grad_input, jnp.sum(grad_output * normed, axis=0), jnp.sum(grad_output, axis=0))


def general_body(
    table,
    token_ids,
    sent_lengths,
    pair_slot,
    pair_lang,
    w_query,
    b_query,
    w_key,
    w_value,
    b_value,
    w_out,
    b_out,
    ln1_gain,
    ln1_bias,
    w_up,
    b_up,
    w_down,
    b_down,
    ln2_gain,
    ln2_bias,
):
    sentences, length = token_ids.shape
    tokens = sentences * length
    vocab_rows, model_width = table.shape
    owners = lax.axis_size(("dp", "fsdp"))
    dp_count = lax.axis_size("dp")
    fsdp_count = lax.axis_size("fsdp")
    capacity = max(2, 2 * tokens // owners)
    device = lax.axis_index(("dp", "fsdp"))
    score_factor = HEAD ** (-0.5)
    flat_ids = token_ids.reshape(tokens)
    owner_of = flat_ids // vocab_rows
    member = (owner_of[:, None] == jnp.arange(owners, dtype=jnp.int32)[None, :]).astype(jnp.int32)
    owner_rank = jnp.sum(jnp.cumsum(member, axis=0) * member, axis=1) - 1
    slot_of = owner_of * capacity + owner_rank
    requests = jnp.full((owners * capacity,), -1, jnp.int32).at[slot_of].set(flat_ids)
    received = lax.all_to_all(
        lax.all_to_all(
            requests.reshape(dp_count, fsdp_count, capacity),
            "dp",
            split_axis=0,
            concat_axis=0,
            tiled=True,
        ),
        "fsdp",
        split_axis=1,
        concat_axis=1,
        tiled=True,
    )
    present = received >= 0
    local_rows = jnp.where(present, received - device * vocab_rows, 0)
    found_rows = jnp.where(present[..., None], table[local_rows], jnp.zeros((), table.dtype))
    replies = lax.all_to_all(
        lax.all_to_all(found_rows, "dp", split_axis=0, concat_axis=0, tiled=True),
        "fsdp",
        split_axis=1,
        concat_axis=1,
        tiled=True,
    )
    embedded = replies.reshape(owners * capacity, model_width)[slot_of]
    gathered = (
        lax.all_gather(w_query, "fsdp", axis=0, tiled=True),
        lax.all_gather(b_query, "fsdp", axis=0, tiled=True),
        lax.all_gather(w_key, "fsdp", axis=0, tiled=True),
        lax.all_gather(w_value, "fsdp", axis=0, tiled=True),
        lax.all_gather(b_value, "fsdp", axis=0, tiled=True),
        lax.all_gather(w_out, "fsdp", axis=0, tiled=True),
        lax.all_gather(b_out, "fsdp", axis=0, tiled=True),
        lax.all_gather(ln1_gain, "fsdp", axis=0, tiled=True),
        lax.all_gather(ln1_bias, "fsdp", axis=0, tiled=True),
        lax.all_gather(w_up, "fsdp", axis=0, tiled=True),
        lax.all_gather(b_up, "fsdp", axis=0, tiled=True),
        lax.all_gather(w_down, "fsdp", axis=0, tiled=True),
        lax.all_gather(b_down, "fsdp", axis=0, tiled=True),
        lax.all_gather(ln2_gain, "fsdp", axis=0, tiled=True),
        lax.all_gather(ln2_bias, "fsdp", axis=0, tiled=True),
    )
    (
        full_wq,
        full_bq,
        full_wk,
        full_wv,
        full_bv,
        full_wo,
        full_bo,
        full_g1,
        full_s1,
        full_wup,
        full_bup,
        full_wdown,
        full_bdown,
        full_g2,
        full_s2,
    ) = gathered
    valid_mask = jnp.arange(length, dtype=jnp.int32)[None, :] < sent_lengths[:, None]
    head_shape = (sentences, length, HEADS, HEAD)
    queries = (jnp.dot(embedded, full_wq, preferred_element_type=jnp.float32) + full_bq).astype(
        jnp.bfloat16
    )
    key_heads = (
        jnp.dot(embedded, full_wk, preferred_element_type=jnp.float32)
        .astype(jnp.bfloat16)
        .reshape(head_shape)
    )
    value_heads = (
        (jnp.dot(embedded, full_wv, preferred_element_type=jnp.float32) + full_bv)
        .astype(jnp.bfloat16)
        .reshape(head_shape)
    )
    query_heads = queries.reshape(head_shape)
    scores = (
        jnp.einsum("bqhd,bkhd->bhqk", query_heads, key_heads, preferred_element_type=jnp.float32)
        * score_factor
    )
    scores = jnp.where(valid_mask[:, None, None, :], scores, MASK_FLOOR)
    row_peak = jnp.max(scores, axis=-1, keepdims=True)
    shifted = jnp.exp(scores - row_peak)
    totals = jnp.sum(shifted, axis=-1, keepdims=True)
    attn_probs = (shifted / totals).astype(jnp.bfloat16)
    context = jnp.einsum(
        "bhqk,bkhd->bqhd", attn_probs, value_heads, preferred_element_type=jnp.float32
    )
    context = context.reshape(tokens, model_width).astype(jnp.bfloat16)
    attended = jnp.dot(context, full_wo, preferred_element_type=jnp.float32) + full_bo
    hidden, normed_one, inverse_one = norm_rows(
        embedded.astype(jnp.float32) + attended, full_g1, full_s1
    )
    hidden_low = hidden.astype(jnp.bfloat16)
    up_pre = jnp.dot(hidden_low, full_wup, preferred_element_type=jnp.float32) + full_bup
    activated = jax.nn.gelu(up_pre, approximate=False).astype(jnp.bfloat16)
    down_pre = jnp.dot(activated, full_wdown, preferred_element_type=jnp.float32) + full_bdown
    normed_out, normed_two, inverse_two = norm_rows(hidden + down_pre, full_g2, full_s2)
    layer_out = jnp.where(valid_mask.reshape(tokens)[:, None], normed_out, 0.0).astype(jnp.bfloat16)
    layer_out = layer_out.reshape(sentences, length, model_width)

    def first_rows(matrix):
        return matrix.reshape(sentences, length, matrix.shape[-1])[:, 0]

    summary = first_rows(normed_out)
    magnitude = jnp.sqrt(jnp.sum(summary * summary, axis=-1, keepdims=True) + EPSILON)
    unit_vector = summary / magnitude
    unit_low = unit_vector.astype(jnp.bfloat16)
    every_unit = lax.all_gather(unit_low, ("dp", "fsdp"), axis=0, tiled=True)
    every_side = pair_slot % 2
    every_pair = pair_slot // 2
    my_slots = lax.dynamic_slice_in_dim(pair_slot, device * sentences, sentences)
    my_side = my_slots % 2
    my_pair = my_slots // 2
    lang_onehot = (pair_lang[:, None] == jnp.arange(LANGS, dtype=jnp.int32)[None, :]).astype(
        jnp.float32
    )
    per_lang = jnp.sum(lang_onehot, axis=0)
    per_pair = 1.0 / (2.0 * LANGS * jnp.sum(lang_onehot * per_lang[None, :], axis=1))
    my_weight = jnp.take(per_pair, my_pair)
    opposite = my_side[:, None] != every_side[None, :]
    partner = opposite & (my_pair[:, None] == every_pair[None, :])
    raw_scores = SCORE_SCALE * contract(unit_low, every_unit, 1, 1)
    pair_scores = jnp.where(partner, raw_scores - SCORE_SCALE * MARGIN_WIDTH, raw_scores)
    pair_scores = jnp.where(opposite, pair_scores, MASK_FLOOR)
    pair_peak = jnp.max(pair_scores, axis=1, keepdims=True)
    pair_exp = jnp.exp(pair_scores - pair_peak)
    pair_total = jnp.sum(pair_exp, axis=1, keepdims=True)
    log_total = pair_peak[:, 0] + jnp.log(pair_total[:, 0])
    picked = jnp.sum(jnp.where(partner, pair_scores, 0.0), axis=1)
    loss_value = lax.psum(jnp.sum(my_weight * (log_total - picked)), ("dp", "fsdp"))
    coefficients = (
        my_weight[:, None] * (pair_exp / pair_total - partner.astype(jnp.float32))
    ).astype(jnp.bfloat16)
    unit_grad = SCORE_SCALE * contract(coefficients, every_unit, 1, 0)
    column_terms = SCORE_SCALE * contract(coefficients, unit_low, 0, 0)
    unit_grad = unit_grad + lax.psum_scatter(
        column_terms, ("dp", "fsdp"), scatter_dimension=0, tiled=True
    )
    along = jnp.sum(unit_vector * unit_grad, axis=-1, keepdims=True)
    summary_grad = (unit_grad - unit_vector * along) / magnitude
    again_weights = (
        lax.all_gather(w_query, "fsdp", axis=0, tiled=True),
        lax.all_gather(w_key, "fsdp", axis=0, tiled=True),
        lax.all_gather(w_value, "fsdp", axis=0, tiled=True),
        lax.all_gather(w_out, "fsdp", axis=0, tiled=True),
        lax.all_gather(ln1_gain, "fsdp", axis=0, tiled=True),
        lax.all_gather(w_up, "fsdp", axis=0, tiled=True),
        lax.all_gather(w_down, "fsdp", axis=0, tiled=True),
        lax.all_gather(ln2_gain, "fsdp", axis=0, tiled=True),
    )
    again_wq, again_wk, again_wv, again_wo, again_g1, again_wup, again_wdown, again_g2 = (
        again_weights
    )
    residual_grad, grad_g2, grad_s2 = norm_back(
        summary_grad, first_rows(normed_two), first_rows(inverse_two), again_g2
    )
    down_grad = residual_grad.astype(jnp.bfloat16)
    activated_cls = first_rows(activated)
    act_grad = contract(down_grad, again_wdown, 1, 1)
    gelu_value, gelu_pull = jax.vjp(partial(jax.nn.gelu, approximate=False), first_rows(up_pre))
    up_grad = gelu_pull(act_grad)[0].astype(jnp.bfloat16)
    hidden_cls = first_rows(hidden_low)
    hidden_grad = contract(up_grad, again_wup, 1, 1) + residual_grad
    first_grad, grad_g1, grad_s1 = norm_back(
        hidden_grad, first_rows(normed_one), first_rows(inverse_one), again_g1
    )
    attend_grad = first_grad.astype(jnp.bfloat16)
    context_cls = first_rows(context)
    context_grad = (
        contract(attend_grad, again_wo, 1, 1).astype(jnp.bfloat16).reshape(sentences, HEADS, HEAD)
    )
    query_cls = query_heads[:, 0]
    cls_scores = (
        jnp.einsum("bhd,bkhd->bhk", query_cls, key_heads, preferred_element_type=jnp.float32)
        * score_factor
    )
    cls_scores = jnp.where(valid_mask[:, None, :], cls_scores, MASK_FLOOR)
    cls_probs = jnp.exp(cls_scores - row_peak[:, :, 0]) / totals[:, :, 0]
    prob_grad = jnp.einsum(
        "bhd,bkhd->bhk", context_grad, value_heads, preferred_element_type=jnp.float32
    )
    score_grad = (
        cls_probs * (prob_grad - jnp.sum(cls_probs * prob_grad, axis=-1, keepdims=True))
    ).astype(jnp.bfloat16)
    query_grad = (
        (
            jnp.einsum("bhk,bkhd->bhd", score_grad, key_heads, preferred_element_type=jnp.float32)
            * score_factor
        )
        .astype(jnp.bfloat16)
        .reshape(sentences, model_width)
    )
    key_grad = (
        (
            jnp.einsum("bhk,bhd->bkhd", score_grad, query_cls, preferred_element_type=jnp.float32)
            * score_factor
        )
        .astype(jnp.bfloat16)
        .reshape(tokens, model_width)
    )
    value_grad = (
        jnp.einsum(
            "bhk,bhd->bkhd",
            cls_probs.astype(jnp.bfloat16),
            context_grad,
            preferred_element_type=jnp.float32,
        )
        .astype(jnp.bfloat16)
        .reshape(tokens, model_width)
    )
    embedded_cls = first_rows(embedded)
    grad_wkey = contract(embedded, key_grad, 0, 0)
    grad_wvalue = contract(embedded, value_grad, 0, 0)
    grad_bvalue = jnp.sum(value_grad, axis=0, dtype=jnp.float32)
    row_grads = contract(key_grad, again_wk, 1, 1) + contract(value_grad, again_wv, 1, 1)
    summary_extra = contract(query_grad, again_wq, 1, 1) + first_grad
    row_grads = (
        row_grads.reshape(sentences, length, model_width)
        .at[:, 0]
        .add(summary_extra)
        .reshape(tokens, model_width)
    )
    outgoing = jnp.zeros((owners * capacity, model_width), jnp.float32).at[slot_of].set(row_grads)
    incoming = lax.all_to_all(
        lax.all_to_all(
            outgoing.reshape(dp_count, fsdp_count, capacity, model_width).astype(jnp.bfloat16),
            "dp",
            split_axis=0,
            concat_axis=0,
            tiled=True,
        ),
        "fsdp",
        split_axis=1,
        concat_axis=1,
        tiled=True,
    ).astype(jnp.float32)
    incoming = jnp.where(
        present.reshape(owners * capacity)[:, None],
        incoming.reshape(owners * capacity, model_width),
        0.0,
    )
    table_grad = (
        jnp.zeros((vocab_rows, model_width), jnp.float32)
        .at[local_rows.reshape(owners * capacity)]
        .add(incoming)
    )
    grad_wquery = contract(embedded_cls, query_grad, 0, 0)
    grad_bquery = jnp.sum(query_grad, axis=0, dtype=jnp.float32)
    grad_wout = contract(context_cls, attend_grad, 0, 0)
    grad_bout = jnp.sum(attend_grad, axis=0, dtype=jnp.float32)
    grad_wup = contract(hidden_cls, up_grad, 0, 0)
    grad_bup = jnp.sum(up_grad, axis=0, dtype=jnp.float32)
    grad_wdown = contract(activated_cls, down_grad, 0, 0)
    grad_bdown = jnp.sum(down_grad, axis=0, dtype=jnp.float32)
    owned_grads = (
        lax.psum_scatter(
            grad_wquery.astype(jnp.bfloat16), "fsdp", scatter_dimension=0, tiled=True
        ).astype(jnp.float32),
        lax.psum_scatter(
            grad_bquery.astype(jnp.bfloat16), "fsdp", scatter_dimension=0, tiled=True
        ).astype(jnp.float32),
        lax.psum_scatter(
            grad_wkey.astype(jnp.bfloat16), "fsdp", scatter_dimension=0, tiled=True
        ).astype(jnp.float32),
        lax.psum_scatter(
            grad_wvalue.astype(jnp.bfloat16), "fsdp", scatter_dimension=0, tiled=True
        ).astype(jnp.float32),
        lax.psum_scatter(
            grad_bvalue.astype(jnp.bfloat16), "fsdp", scatter_dimension=0, tiled=True
        ).astype(jnp.float32),
        lax.psum_scatter(
            grad_wout.astype(jnp.bfloat16), "fsdp", scatter_dimension=0, tiled=True
        ).astype(jnp.float32),
        lax.psum_scatter(
            grad_bout.astype(jnp.bfloat16), "fsdp", scatter_dimension=0, tiled=True
        ).astype(jnp.float32),
        lax.psum_scatter(
            grad_g1.astype(jnp.bfloat16), "fsdp", scatter_dimension=0, tiled=True
        ).astype(jnp.float32),
        lax.psum_scatter(
            grad_s1.astype(jnp.bfloat16), "fsdp", scatter_dimension=0, tiled=True
        ).astype(jnp.float32),
        lax.psum_scatter(
            grad_wup.astype(jnp.bfloat16), "fsdp", scatter_dimension=0, tiled=True
        ).astype(jnp.float32),
        lax.psum_scatter(
            grad_bup.astype(jnp.bfloat16), "fsdp", scatter_dimension=0, tiled=True
        ).astype(jnp.float32),
        lax.psum_scatter(
            grad_wdown.astype(jnp.bfloat16), "fsdp", scatter_dimension=0, tiled=True
        ).astype(jnp.float32),
        lax.psum_scatter(
            grad_bdown.astype(jnp.bfloat16), "fsdp", scatter_dimension=0, tiled=True
        ).astype(jnp.float32),
        lax.psum_scatter(
            grad_g2.astype(jnp.bfloat16), "fsdp", scatter_dimension=0, tiled=True
        ).astype(jnp.float32),
        lax.psum_scatter(
            grad_s2.astype(jnp.bfloat16), "fsdp", scatter_dimension=0, tiled=True
        ).astype(jnp.float32),
    )
    summed = (
        lax.psum(owned_grads[0].astype(jnp.bfloat16), "dp").astype(jnp.float32),
        lax.psum(owned_grads[1].astype(jnp.bfloat16), "dp").astype(jnp.float32),
        lax.psum(owned_grads[2].astype(jnp.bfloat16), "dp").astype(jnp.float32),
        lax.psum(owned_grads[3].astype(jnp.bfloat16), "dp").astype(jnp.float32),
        lax.psum(owned_grads[4].astype(jnp.bfloat16), "dp").astype(jnp.float32),
        lax.psum(owned_grads[5].astype(jnp.bfloat16), "dp").astype(jnp.float32),
        lax.psum(owned_grads[6].astype(jnp.bfloat16), "dp").astype(jnp.float32),
        lax.psum(owned_grads[7].astype(jnp.bfloat16), "dp").astype(jnp.float32),
        lax.psum(owned_grads[8].astype(jnp.bfloat16), "dp").astype(jnp.float32),
        lax.psum(owned_grads[9].astype(jnp.bfloat16), "dp").astype(jnp.float32),
        lax.psum(owned_grads[10].astype(jnp.bfloat16), "dp").astype(jnp.float32),
        lax.psum(owned_grads[11].astype(jnp.bfloat16), "dp").astype(jnp.float32),
        lax.psum(owned_grads[12].astype(jnp.bfloat16), "dp").astype(jnp.float32),
        lax.psum(owned_grads[13].astype(jnp.bfloat16), "dp").astype(jnp.float32),
        lax.psum(owned_grads[14].astype(jnp.bfloat16), "dp").astype(jnp.float32),
    )
    return (
        layer_out,
        loss_value,
        table_grad,
        summed[0],
        summed[1],
        summed[2],
        summed[3],
        summed[4],
        summed[5],
        summed[6],
        summed[7],
        summed[8],
        summed[9],
        summed[10],
        summed[11],
        summed[12],
        summed[13],
        summed[14],
    )


CORES = 2
PLANES = 4
LINES = 4
CHIPS = PLANES * LINES
DEVICES = CORES * CHIPS
CAPACITY = 48
GROUPS = 3
PAD = 16
TOKENS = 768
WIDTH = 768
WIDE = 3072
VOCAB_ROWS = 1024
PAIR_ROWS = HEADS * PAD
SLOT_ROWS = DEVICES * PAD
LONG = 64
BLOCK = 256
MESH = pl.DeviceIdType.MESH
LOW = jnp.bfloat16
FULL = jnp.float32
VMEM_LIMIT = 62 * 1024 * 1024

INPUTS = ["table", "token_ids", "lens", "slots", "langs"]
INPUTS += ["wq", "bq", "wk", "wv", "bv", "wo", "bo", "g1", "s1", "wup", "bup", "wdown", "bdown"]
INPUTS += ["g2", "s2"]
OUTPUTS = ["layer_out", "table_grad", "g_wq", "g_wk", "g_wv", "g_wo", "g_wup", "g_wdown"]
OUTPUTS += ["g_small", "loss"]


def place():
    core = lax.axis_index("dp")
    chip = lax.axis_index("fsdp")
    along_x = chip + 1 - 2 * (chip % 2)
    along_y = chip + 2 - 4 * ((chip // 2) % 2)
    first = along_x + core * (along_y - along_x)
    second = along_y + core * (along_x - along_y)
    return core, chip, first, second


def greet():
    core, chip, _, _ = place()
    me = core * CHIPS + chip
    barrier = pltpu.get_barrier_semaphore()

    def signal(step):
        other = lax.rem(me + step, DEVICES)
        pl.semaphore_signal(
            barrier,
            inc=1,
            device_id=(lax.div(other, CHIPS), lax.rem(other, CHIPS)),
            device_id_type=MESH,
        )

    every(1, DEVICES, signal)


def enter():
    pl.semaphore_wait(pltpu.get_barrier_semaphore(), DEVICES - 1)


def remote(source, target, send_sem, recv_sem, core, chip):
    return pltpu.make_async_remote_copy(
        src_ref=source,
        dst_ref=target,
        send_sem=send_sem,
        recv_sem=recv_sem,
        device_id=(core, chip),
        device_id_type=MESH,
    )


def every(start, stop, act):
    def step(index, carry):
        act(index)
        return carry

    lax.fori_loop(start, stop, step, 0)


def weight_steps(piece, many, send, recv):
    core, chip, first, second = place()
    plane, line = chip // LINES, chip % LINES
    line_first, line_second = first % LINES, second % LINES
    line_far = line_first + line_second - line
    is_low, is_high = plane > 0, plane < PLANES - 1

    def copy(send_index, recv_index, at, to_core, to_chip, carried=core):
        part = piece(at, carried)
        return remote(part, part, send.at[send_index], recv.at[recv_index], to_core, to_chip)

    def up(at_plane):
        return copy(at_plane, at_plane, at_plane * LINES + line, core, chip + LINES)

    def down(at_plane, index):
        return copy(index, at_plane, at_plane * LINES + line, core, chip - LINES)

    def side(at_plane, base, at_line, target):
        return copy(5, base + at_plane, at_plane * LINES + at_line, core, target)

    def across(at_plane, at_line):
        return copy(6, 17, at_plane * LINES + at_line, 1 - core, chip)

    def all_of(count, send_index, recv_index):
        part = many(count)
        return remote(part, part, send.at[send_index], recv.at[recv_index], 1 - core, chip)

    def begin():
        pl.when(is_high)(lambda: up(plane).start())
        pl.when(is_low)(lambda: down(plane, PLANES).start())
        side(plane, 5, line, first).start()
        side(plane, 9, line, second).start()

    def at_distance(distance, act):
        if distance == 0:
            act(plane, None)
            return
        pl.when(plane >= distance)(lambda: act(plane - distance, True))
        pl.when(plane + distance < PLANES)(lambda: act(plane + distance, False))

    def chain(distance):
        def act(at_plane, from_low):
            if from_low:
                up(at_plane).wait_recv()
                pl.when(is_high)(lambda: up(at_plane).start())
            else:
                down(at_plane, at_plane).wait_recv()
                pl.when(is_low)(lambda: down(at_plane, at_plane).start())
            side(at_plane, 5, line, first).start()
            side(at_plane, 9, line, second).start()
            across(at_plane, line).start()

        return partial(at_distance, distance, act)

    def near(distance):
        def act(at_plane, from_low):
            side(at_plane, 5, line_first, first).wait_recv()
            side(at_plane, 13, line_first, second).start()
            across(at_plane, line_first).start()

        return partial(at_distance, distance, act)

    def far(distance):
        def act(at_plane, from_low):
            side(at_plane, 9, line_second, second).wait_recv()
            across(at_plane, line_second).start()
            side(at_plane, 13, line_far, second).wait_recv()
            across(at_plane, line_far).start()

        return partial(at_distance, distance, act)

    def finish():
        all_of(15, 6, 17).wait_recv()

    def drain():
        def sent(index):
            copy(index, index, chip, 1 - core, chip).wait_send()

        for at_plane in range(PLANES):
            pl.when((plane >= at_plane) & is_high)(partial(sent, at_plane))
            pl.when((plane < at_plane) & is_low)(partial(sent, at_plane))
        pl.when(is_low)(partial(sent, PLANES))
        all_of(12, 5, 17).wait_send()
        all_of(15, 6, 17).wait_send()

    moves = [chain(1), near(0), chain(2), near(1), chain(3), far(0)]
    moves += [near(2), far(1), near(3), far(2), far(3)]
    return begin, moves, finish, drain


def gather_steps(buffer, send, recv):
    core, chip, first, second = place()
    plane, line = chip // LINES, chip % LINES
    line_first, line_second = first % LINES, second % LINES
    line_far = line_first + line_second - line
    half = buffer.shape[-1] // 2
    columns = pl.ds(pl.multiple_of(core * half, 128), half)
    others = pl.ds(pl.multiple_of((1 - core) * half, 128), half)

    def copy(index, part, to_core, to_chip):
        return remote(part, part, send.at[index], recv.at[index], to_core, to_chip)

    def own(at):
        return buffer.at[at, plane, line]

    def chip_part(at_plane, at_line, which):
        return buffer.at[:, at_plane, at_line, :, which]

    def line_part(at_line, which):
        return buffer.at[:, :, at_line, :, which]

    def start():
        copy(0, own(core), 1 - core, chip).start()

    def planes():
        copy(0, own(1 - core), 1 - core, chip).wait_recv()
        for step in range(1, PLANES):
            part = chip_part(plane, line, columns)
            copy(step, part, core, (chip + LINES * step) % CHIPS).start()

    def sides():
        for step in range(1, PLANES):
            part = chip_part((plane + PLANES - step) % PLANES, line, columns)
            copy(step, part, core, chip).wait_recv()
        copy(4, line_part(line, columns), core, first).start()
        copy(5, line_part(line, columns), core, second).start()
        for step in range(1, PLANES):
            part = chip_part((plane + PLANES - step) % PLANES, line, columns)
            copy(6 + step, part, 1 - core, chip).start()

    def corner():
        copy(4, line_part(line_first, columns), core, first).wait_recv()
        copy(6, line_part(line_first, columns), core, second).start()
        copy(10, line_part(line_first, columns), 1 - core, chip).start()
        copy(5, line_part(line_second, columns), core, second).wait_recv()
        copy(11, line_part(line_second, columns), 1 - core, chip).start()

    def last():
        copy(6, line_part(line_far, columns), core, second).wait_recv()
        copy(12, line_part(line_far, columns), 1 - core, chip).start()

    def finish():
        for step in range(1, PLANES):
            part = chip_part((plane + PLANES - step) % PLANES, line, others)
            copy(6 + step, part, 1 - core, chip).wait_recv()
        copy(10, line_part(line_second, others), 1 - core, chip).wait_recv()
        copy(11, line_part(line_first, others), 1 - core, chip).wait_recv()
        copy(12, line_part(line_far, others), 1 - core, chip).wait_recv()

    def drain():
        copy(0, own(core), 1 - core, chip).wait_send()
        for index in [1, 2, 3, 7, 8, 9]:
            copy(index, chip_part(plane, line, columns), 1 - core, chip).wait_send()
        for index in [4, 5, 6, 10, 11, 12]:
            copy(index, line_part(line, columns), 1 - core, chip).wait_send()

    return [start, planes, sides, corner, last, finish], drain


def iota(shape, axis):
    return lax.broadcasted_iota(jnp.int32, shape, axis)


def over(numbers, power):
    return lax.shift_right_arithmetic(numbers, jnp.full_like(numbers, power.bit_length() - 1))


def within(numbers, power):
    return numbers & (power - 1)


def as_column(row):
    parts = []
    for start in range(0, row.shape[1], 128):
        tile = jnp.broadcast_to(row[:, start : start + 128], (128, 128))
        parts.append(jnp.transpose(tile)[:, 0:1])
    return jnp.concatenate(parts, axis=0)


def as_row(column):
    parts = []
    for start in range(0, column.shape[0], 128):
        tile = jnp.broadcast_to(column[start : start + 128, :], (128, 128))
        parts.append(jnp.transpose(tile)[0:1, :])
    return jnp.concatenate(parts, axis=1)


def dot(left_side, right_side):
    return contract(left_side, right_side, 1, 0)


def dot_turned(left_side, right_side):
    return contract(left_side, right_side, 1, 1)


def norm_parts(inputs):
    centered = inputs - jnp.mean(inputs, axis=-1, keepdims=True)
    inverse = lax.rsqrt(jnp.mean(centered * centered, axis=-1, keepdims=True) + EPSILON)
    return centered * inverse, inverse


def norm_back_parts(grad_output, normed, inverse, ln_gain):
    grad_normed = grad_output * ln_gain
    first_term = jnp.mean(grad_normed, axis=-1, keepdims=True)
    second_term = jnp.mean(grad_normed * normed, axis=-1, keepdims=True)
    return (
        inverse * (grad_normed - first_term - normed * second_term),
        jnp.sum(grad_output * normed, axis=0, keepdims=True),
        jnp.sum(grad_output, axis=0, keepdims=True),
    )


def erf_parts(inputs):
    decay = jnp.exp(-0.5 * inputs * inputs)
    share = 1.0 / (1.0 + jnp.abs(inputs) * (0.3275911 * 0.5**0.5))
    terms = [1.061405429, -1.453152027, 1.421413741, -0.284496736, 0.254829592]
    series = 0.5 * terms[0]
    for term in terms[1:]:
        series = series * share + 0.5 * term
    tail = series * share * decay
    return jnp.where(inputs >= 0.0, 1.0 - tail, tail), decay


def gelu_parts(inputs):
    below, decay = erf_parts(inputs)
    return inputs * below, below + inputs * decay * ((2.0 * 3.141592653589793) ** -0.5)


def gelu(inputs):
    return inputs * erf_parts(inputs)[0]


def layer_kernel(names, *refs):
    r = SimpleNamespace(**dict(zip(names, refs, strict=True)))
    core, chip, _, _ = place()
    me = core * CHIPS + chip
    here = (core, chip // LINES, chip % LINES)
    scale = HEAD ** (-0.5)
    depth, deep = WIDTH // CHIPS, WIDE // CHIPS
    sentences = TOKENS // LONG

    for j in range(TOKENS // 128):
        r.ids[j : j + 1, :] = jnp.concatenate(
            [r.token_ids[2 * j : 2 * j + 1, :], r.token_ids[2 * j + 1 : 2 * j + 2, :]], axis=1
        )
    r.ids[TOKENS // 128 : 8, :] = jnp.zeros((8 - TOKENS // 128, 128), jnp.int32)
    greet()
    ahead = (iota((TOKENS, TOKENS), 0) < iota((TOKENS, TOKENS), 1)).astype(LOW)
    r.embedded[...] = ahead
    mine = pl.ds(pl.multiple_of(chip * depth, 16), depth)
    for index, shard in enumerate([r.wq, r.wk, r.wv, r.wo]):
        r.wa[mine, index * WIDTH : (index + 1) * WIDTH] = shard[...]
    r.wb[mine, :] = r.wup[...]
    r.wc[pl.ds(pl.multiple_of(chip * deep, 16), deep), :] = r.wdown[...]
    r.every_ids[me] = r.ids[...]
    enter()

    def peer(step):
        other = lax.rem(me + step, DEVICES)
        return other, lax.div(other, CHIPS), lax.rem(other, CHIPS)

    def ids_copy(step):
        other, to_core, to_chip = peer(step)
        return remote(r.ids, r.every_ids.at[me], r.one_send.at[0], r.one_recv.at[0], to_core, to_chip)

    def all_but_one(ref, index):
        part = ref.at[0 : DEVICES - 1]
        return remote(part, part, r.one_send.at[index], r.one_recv.at[index], 1 - core, chip)

    every(1, DEVICES, lambda step: ids_copy(step).start())

    def block(ref, rows, columns):
        def piece(at, carried):
            return ref.at[
                pl.ds(pl.multiple_of(at * rows, 16), rows),
                pl.ds(pl.multiple_of(carried * columns, 128), columns),
            ]

        def many(count):
            return ref.at[0 : count * rows, 0:columns]

        return piece, many

    begin_a, moves_a, finish_a, drain_a = weight_steps(
        *block(r.wa, depth, 2 * WIDTH), r.weight_send.at[0], r.weight_recv.at[0]
    )
    begin_b, moves_b, finish_b, drain_b = weight_steps(
        *block(r.wb, depth, WIDE // 2), r.weight_send.at[1], r.weight_recv.at[1]
    )
    begin_c, moves_c, finish_c, drain_c = weight_steps(
        *block(r.wc, deep, WIDTH // 2), r.weight_send.at[2], r.weight_recv.at[2]
    )
    begin_a()
    begin_b()

    def move(*steps):
        for moves, first_step in steps:
            moves[first_step]()
            moves[first_step + 1]()

    all_but_one(r.every_ids, 0).wait_recv()
    all_ids = jnp.concatenate([r.every_ids[:, j, :] for j in range(TOKENS // 128)], axis=1)
    all_owner = over(all_ids, VOCAB_ROWS)
    asked = all_owner == me
    ranks = dot(asked.astype(LOW), r.embedded[...])
    r.rank[...] = jnp.where(asked, ranks, -1.0)
    local_row = (all_ids - all_owner * VOCAB_ROWS + 1).astype(FULL)
    r.code[...] = local_row + (over(iota((DEVICES, TOKENS), 1), LONG) * 2048).astype(FULL)

    quarter_size = DEVICES // 4

    def rows_copy(other, quarter):
        return remote(
            r.rows.at[:, pl.ds(pl.multiple_of(other * PAD, 16), PAD), :],
            r.replies.at[:, pl.ds(pl.multiple_of(me * PAD, 16), PAD), :],
            r.rows_send.at[quarter],
            r.rows_recv.at[quarter],
            lax.div(other, CHIPS),
            lax.rem(other, CHIPS),
        )

    def rows_of(quarter):
        count = quarter_size - 1 if quarter == 3 else quarter_size
        part = r.replies.at[:, 0 : count * PAD, :]
        return remote(
            part, part, r.rows_send.at[quarter], r.rows_recv.at[quarter], 1 - core, chip
        )

    def pick(source):
        rank = r.rank[pl.ds(source, 1), :]
        code = r.code[pl.ds(source, 1), :]
        here_at = iota((CAPACITY, TOKENS), 0).astype(FULL) == rank
        found = jnp.sum(jnp.where(here_at, code, 0.0), axis=1, keepdims=True)
        sent = jnp.floor(found * (1.0 / 2048))
        row = found - sent * 2048.0 - 1.0
        chosen = (iota((CAPACITY, VOCAB_ROWS), 1).astype(FULL) == row).astype(LOW)
        at = pl.ds(pl.multiple_of(source * PAD, 16), PAD)
        source_sent = sent + (source * PAD).astype(FULL)
        for group in range(GROUPS):
            part = slice(group * PAD, (group + 1) * PAD)
            r.chosen[group, at, :] = chosen[part]
            r.found[group, at, 0:1] = row[part]
            r.found[group, at, 1:2] = source_sent[part]

    def quarter_rows(quarter):
        now = lax.rem(lax.div(me, quarter_size) + 1 + quarter, 4)

        def pick_two(index):
            pick(now * quarter_size + 2 * index)
            pick(now * quarter_size + 2 * index + 1)

        every(0, quarter_size // 2, pick_two)
        span = pl.ds(pl.multiple_of(now * quarter_size * PAD, 128), quarter_size * PAD)
        for start in range(0, WIDTH, BLOCK):
            lanes = slice(start, start + BLOCK)
            picked = r.chosen[:, span, :].reshape(GROUPS * quarter_size * PAD, VOCAB_ROWS)
            found_rows = dot(picked, r.table[:, lanes]).astype(LOW)
            r.rows[:, span, lanes] = found_rows.reshape(GROUPS, quarter_size * PAD, BLOCK)

        def send(index):
            other = now * quarter_size + lax.rem(lax.rem(me, quarter_size) + index, quarter_size)
            rows_copy(other, quarter).start()

        every(lax.div(quarter, 3), quarter_size, send)
        pl.when(quarter == 0)(partial(move, (moves_a, 0)))
        pl.when(quarter == 1)(partial(move, (moves_b, 0)))
        pl.when(quarter == 2)(partial(move, (moves_a, 2)))
        pl.when(quarter == 3)(partial(move, (moves_b, 2)))

    every(0, 4, quarter_rows)
    begin_c()
    own_at = pl.ds(pl.multiple_of(me * PAD, 16), PAD)
    r.replies[:, own_at, :] = r.rows[:, own_at, :]

    move((moves_a, 4))

    small_here = pl.ds(pl.multiple_of(chip * 128, 128), 128)
    lines = [r.bq, r.bv, r.bo, r.g1, r.s1, r.bdown, r.g2, r.s2]
    lines = [line[...].reshape(1, depth).astype(FULL) for line in lines]
    up_line = r.bup[...].reshape(1, deep).astype(FULL)
    lines += [up_line[:, part * depth : (part + 1) * depth] for part in range(deep // depth)]
    lines.append(jnp.zeros((PAD - len(lines), depth), FULL))
    own_small = jnp.concatenate(lines, axis=0)
    own_small = jnp.concatenate([own_small, jnp.zeros((PAD, 128 - depth), FULL)], axis=1)
    r.smalls[:, small_here] = own_small.astype(LOW)

    def small_copy(step):
        part = r.smalls.at[:, small_here]
        to_chip = lax.rem(chip + step, CHIPS)
        return remote(part, part, r.small_send.at[0], r.small_recv.at[0], core, to_chip)

    def all_smalls():
        part = r.smalls.at[:, 0 : (CHIPS - 1) * 128]
        return remote(part, part, r.small_send.at[0], r.small_recv.at[0], 1 - core, chip)

    every(1, CHIPS, lambda step: small_copy(step).start())
    move((moves_b, 4))

    own_row = jnp.concatenate([r.ids[j : j + 1, :] for j in range(TOKENS // 128)], axis=1)
    owner_row = over(own_row, VOCAB_ROWS).astype(FULL)
    owner_col = as_column(owner_row)
    earlier = (owner_row == owner_col) & (iota((TOKENS, TOKENS), 1) < iota((TOKENS, TOKENS), 0))
    own_rank = jnp.sum(earlier.astype(FULL), axis=1, keepdims=True)
    own_group = jnp.floor(own_rank * (1.0 / PAD))
    own_slot = own_group * SLOT_ROWS + owner_col * PAD + (own_rank - own_group * PAD)
    r.slot_col[...] = own_slot
    r.slot_line[0:1, :] = as_row(own_slot)
    move((moves_a, 6), (moves_c, 0))

    at_sent = over(iota((1, TOKENS), 1), LONG)
    lens = jnp.concatenate(
        [r.lens[...].reshape(1, sentences).astype(FULL), jnp.zeros((1, PAD - sentences), FULL)],
        axis=1,
    )
    spread_lens = dot(
        jnp.broadcast_to(lens, (8, PAD)).astype(LOW),
        (iota((PAD, TOKENS), 0) == over(iota((PAD, TOKENS), 1), LONG)).astype(LOW),
    )[0:1]
    valid_row = ((iota((1, TOKENS), 1) - at_sent * LONG).astype(FULL) < spread_lens).astype(FULL)
    r.valid_line[0:1, :] = valid_row
    r.valid_col[...] = as_column(valid_row)
    half_block = BLOCK // 2
    stacked_shape = (4 * half_block, half_block)
    same = within(over(iota(stacked_shape, 0), LONG), 2) == over(iota(stacked_shape, 1), LONG)
    r.block_bias[...] = jnp.where(same, 0.0, MASK_FLOOR)
    r.valid_bias[0:1, :] = (1.0 - valid_row) * MASK_FLOOR

    slots = r.slots[...].reshape(1, DEVICES * sentences)
    gap = jnp.full((1, PAD - sentences), -2, jnp.int32)
    slot_line = jnp.concatenate(
        [
            part
            for device in range(DEVICES)
            for part in (slots[:, device * sentences : (device + 1) * sentences], gap)
        ],
        axis=1,
    )
    side_line = within(slot_line, 2) + jnp.where(slot_line < 0, 8, 0)
    pair_line = over(slot_line, 2)
    pairs = r.langs.shape[0]
    lang_line = r.langs[...].reshape(1, pairs).astype(FULL)
    lang_line = jnp.concatenate([lang_line, jnp.full((1, -pairs % 128), -1.0, FULL)], axis=1)
    lang_col = as_column(lang_line)
    same_lang = jnp.sum(jnp.where(lang_col == lang_line, 1.0, 0.0), axis=1, keepdims=True)
    per_pair = 1.0 / (2.0 * LANGS * same_lang)
    at_pair = iota((lang_line.shape[1], SLOT_ROWS), 0) == pair_line
    weight_line = jnp.sum(jnp.where(at_pair, per_pair, 0.0), axis=0, keepdims=True)
    r.pairs[0:1, :] = weight_line
    r.pairs[1:2, :] = pair_line.astype(FULL)
    r.pairs[2:3, :] = side_line.astype(FULL)
    r.pairs_col[:, 0:1] = as_column(weight_line)
    r.pairs_col[:, 1:2] = as_column(pair_line.astype(FULL))
    r.pairs_col[:, 2:3] = as_column(side_line.astype(FULL))
    move((moves_b, 6), (moves_c, 2))

    all_smalls().wait_recv()
    smalls = r.smalls[...].astype(FULL)
    r.vectors[:, 0:WIDTH] = jnp.concatenate(
        [smalls[:, at * 128 : at * 128 + depth] for at in range(CHIPS)], axis=1
    )
    r.up_bias[0:1, :] = jnp.concatenate(
        [
            smalls[8 + part : 9 + part, at * 128 : at * 128 + depth]
            for at in range(CHIPS)
            for part in range(deep // depth)
        ],
        axis=1,
    )

    def vector(index):
        return r.vectors[index : index + 1, :]

    r.qkv_bias[0:1, 0:WIDTH] = vector(0)
    r.qkv_bias[0:1, WIDTH : 2 * WIDTH] = jnp.zeros((1, WIDTH), FULL)
    r.qkv_bias[0:1, 2 * WIDTH : 3 * WIDTH] = vector(1)

    move((moves_a, 8), (moves_b, 8), (moves_c, 4))

    def first_row(source):
        code = jnp.where(r.rank[pl.ds(source, 1), :] >= 0.0, r.code[pl.ds(source, 1), :], 0.0)
        at_first = iota((PAD, TOKENS), 1) == iota((PAD, TOKENS), 0) * LONG
        found = jnp.sum(jnp.where(at_first, code, 0.0), axis=1, keepdims=True)
        row = found - jnp.floor(found * (1.0 / 2048)) * 2048.0 - 1.0
        r.found[GROUPS, pl.ds(pl.multiple_of(source * PAD, 16), PAD), 0:1] = row

    every(0, DEVICES, first_row)
    for group in range(GROUPS + 1):
        named = as_row(r.found[group, :, 0:1])
        by_row = iota((VOCAB_ROWS, SLOT_ROWS), 0).astype(FULL) == named
        r.by_row[:, group * SLOT_ROWS : (group + 1) * SLOT_ROWS] = by_row.astype(LOW)

    def order(tile):
        at = pl.ds(pl.multiple_of(tile * BLOCK, BLOCK), BLOCK)
        lanes = iota((BLOCK, GROUPS * SLOT_ROWS), 1).astype(FULL)
        r.qkv[at, 0 : GROUPS * SLOT_ROWS] = (r.slot_col[at, :] == lanes).astype(LOW)

    every(0, TOKENS // BLOCK, order)
    for group in range(GROUPS):
        slot_at = iota((SLOT_ROWS, TOKENS), 0) + group * SLOT_ROWS
        named = (slot_at.astype(FULL) == r.slot_line[0:1, :]).astype(LOW)
        r.slot_hot[group] = named
    moves_a[10]()
    moves_b[10]()
    finish_a()
    for quarter in range(4):
        rows_of(quarter).wait_recv()

    def embed(tile):
        at = pl.ds(pl.multiple_of(tile * BLOCK, BLOCK), BLOCK)
        replies = r.replies[:, :, at].reshape(GROUPS * SLOT_ROWS, BLOCK)
        r.embedded[:, at] = dot(r.qkv[:, 0 : GROUPS * SLOT_ROWS], replies).astype(LOW)

    every(0, WIDTH // BLOCK, embed)

    def project(tile):
        at = pl.ds(pl.multiple_of(tile * BLOCK, BLOCK), BLOCK)
        r.qkv[:, at] = (dot(r.embedded[...], r.wa[:, at]) + r.qkv_bias[0:1, at]).astype(LOW)

    move((moves_c, 6))
    every(0, 9, project)

    row_sent = within(iota((PAIR_ROWS, WIDTH), 0), PAD)
    row_head = over(iota((PAIR_ROWS, WIDTH), 0), PAD)
    lane_block = over(iota((PAIR_ROWS, WIDTH), 1), HEAD)
    in_head = row_head == lane_block
    seen = (row_sent == lane_block) & (r.valid_line[0:1, :] > 0.0)
    firsts = (iota((PAD, TOKENS), 1) == iota((PAD, TOKENS), 0) * LONG).astype(LOW)
    real_row = iota((PAD, 1), 0) < sentences

    def spread(rows):
        return jnp.where(in_head, jnp.concatenate([rows] * HEADS, axis=0), jnp.zeros((), LOW))

    def fold(tall):
        tall = jnp.where(in_head, tall, 0.0)
        return sum(tall[head * PAD : (head + 1) * PAD] for head in range(HEADS))

    keys, values = slice(WIDTH, 2 * WIDTH), slice(2 * WIDTH, 3 * WIDTH)
    embedded_cls = dot(firsts, r.embedded[...]).astype(LOW)
    query_cls = (dot(embedded_cls, r.wa[:, 0:WIDTH]) + vector(0)).astype(LOW)
    cls_scores = dot_turned(spread(query_cls), r.qkv[:, keys]) * scale
    cls_scores = jnp.where(seen, cls_scores, MASK_FLOOR)
    cls_peak = jnp.max(cls_scores, axis=1, keepdims=True)
    cls_exp = jnp.where(seen, jnp.exp(cls_scores - cls_peak), 0.0)
    cls_total = jnp.sum(cls_exp, axis=1, keepdims=True)
    cls_probs = cls_exp / jnp.where(cls_total > 0.0, cls_total, 1.0)
    probs_low = cls_probs.astype(LOW)
    r.probs[...] = cls_probs
    context_cls = fold(dot(probs_low, r.qkv[:, values])).astype(LOW)
    first_cls = (
        embedded_cls.astype(FULL)
        + dot(context_cls, r.wa[:, 3 * WIDTH : 4 * WIDTH])
        + vector(2)
    )
    normed_one, inverse_one = norm_parts(first_cls)
    r.normed_one[...] = normed_one
    hidden_cls = normed_one * vector(3) + vector(4)
    hidden_cls_low = hidden_cls.astype(LOW)
    early_here = r.early.at[here]
    early_here[:, 0:WIDTH] = hidden_cls_low
    early_here[:, WIDTH : 2 * WIDTH] = query_cls
    steps_u, drain_u = gather_steps(r.units, r.gather_send.at[0], r.gather_recv.at[0])
    steps_e, drain_e = gather_steps(r.early, r.gather_send.at[1], r.gather_recv.at[1])
    steps_d, drain_d = gather_steps(r.downs, r.gather_send.at[2], r.gather_recv.at[2])
    steps_a, drain_a2 = gather_steps(r.attends, r.gather_send.at[3], r.gather_recv.at[3])
    steps_q, drain_q = gather_steps(r.queries, r.gather_send.at[4], r.gather_recv.at[4])
    steps_e[0]()

    def attend(unit):
        rows = pl.ds(pl.multiple_of(unit * half_block, half_block), half_block)
        lane_head = over(iota((half_block, BLOCK), 1), HEAD)
        bias = r.block_bias[...] + r.valid_bias[0:1, rows]

        def part(which, lane):
            return r.qkv[rows, which * WIDTH + lane : which * WIDTH + lane + BLOCK]

        for lane in range(0, WIDTH, BLOCK):
            query = part(0, lane) * jnp.asarray(scale, LOW)
            key, value = part(1, lane), part(2, lane)
            stacked = jnp.concatenate(
                [jnp.where(lane_head == head, query, jnp.zeros((), LOW)) for head in range(4)],
                axis=0,
            )
            scores = dot_turned(stacked, key) + bias
            shifted = jnp.exp(scores - jnp.max(scores, axis=1, keepdims=True))
            probs = shifted * (1.0 / jnp.sum(shifted, axis=1, keepdims=True))
            mixed = dot(probs.astype(LOW), value)
            result = mixed[0:half_block]
            for head in range(1, 4):
                result = jnp.where(
                    lane_head == head, mixed[head * half_block : (head + 1) * half_block], result
                )
            r.context[rows, lane : lane + BLOCK] = result.astype(LOW)

    def open_tile(tile):
        at = pl.ds(pl.multiple_of(tile * BLOCK, BLOCK), BLOCK)
        attended = dot(r.context[at, :], r.wa[:, 3 * WIDTH : 4 * WIDTH]) + vector(2)
        normed, _ = norm_parts(r.embedded[at, :].astype(FULL) + attended)
        hidden = normed * vector(3) + vector(4)
        r.context[at, :] = hidden.astype(LOW)
        r.table_full[at, :] = hidden + vector(5)

    most = SLOT_ROWS
    rest_at = pl.ds(most, TOKENS - most)

    def up_product(part):
        at = pl.ds(pl.multiple_of(part * BLOCK, BLOCK), BLOCK)
        return dot(r.context[...], r.wb[:, at]) + r.up_bias[0:1, at]

    def feed_up(part, last=False):
        active = gelu(r.tile_up[...]).astype(LOW)
        if not last:
            r.tile_up[...] = up_product(part + 1)
        lanes = pl.ds(pl.multiple_of(lax.rem(part, 4) * BLOCK, BLOCK), BLOCK)
        r.chosen[lax.div(part, 4), :, lanes] = active[:most]
        rest = pl.ds(pl.multiple_of(lax.div(part, 6) * BLOCK, BLOCK), BLOCK)
        lanes = pl.ds(pl.multiple_of(lax.rem(part, 6) * BLOCK, BLOCK), BLOCK)
        r.slopes[rest, lanes] = active[most:]

    def feed_down(part):
        lanes = pl.ds(pl.multiple_of(part * BLOCK, BLOCK), BLOCK)
        total = r.table_full[0:most, lanes]
        for group in range(GROUPS):
            rows = slice(group * VOCAB_ROWS, (group + 1) * VOCAB_ROWS)
            total = total + dot(r.chosen[group], r.wc[rows, lanes])
        r.table_full[0:most, lanes] = total

    def feed_rest(part):
        lanes = pl.ds(pl.multiple_of(part * BLOCK, BLOCK), BLOCK)
        low_part = dot(r.slopes[0:BLOCK, :], r.wc[0 : WIDE // 2, lanes])
        high_part = dot(r.slopes[BLOCK : 2 * BLOCK, :], r.wc[WIDE // 2 :, lanes])
        r.table_full[rest_at, lanes] += low_part + high_part

    def layer_copy(tile):
        at = pl.ds(pl.multiple_of(tile * BLOCK, BLOCK), BLOCK)
        return pltpu.make_async_copy(r.context.at[at], r.layer_out.at[at], r.out_sem.at[tile])

    def close_tile(tile):
        at = pl.ds(pl.multiple_of(tile * BLOCK, BLOCK), BLOCK)
        normed, _ = norm_parts(r.table_full[at, :])
        out = normed * vector(6) + vector(7)
        r.context[at, :] = (out * r.valid_col[at, :]).astype(LOW)
        layer_copy(tile).start()

    finish_b()
    r.hidden_cls[...] = hidden_cls_low

    def up_part(part):
        at = pl.ds(pl.multiple_of(part * WIDTH, BLOCK), WIDTH)
        active, slope = gelu_parts(dot(r.hidden_cls[...], r.wb[:, at]) + r.up_bias[0:1, at])
        r.active_cls[:, at] = active.astype(LOW)
        r.slope_cls[:, at] = slope

    every(0, WIDE // WIDTH, up_part)
    steps_e[1]()

    def attend_step(unit):
        attend(unit)
        pl.when(unit == 1)(partial(move, (moves_c, 8)))
        pl.when(unit == 3)(moves_c[10])
        pl.when(unit == 4)(steps_e[2])

    every(0, 6, attend_step)
    finish_c()

    def pack_tall(target, first_row, act):
        def run(part):
            window = jnp.minimum(lax.div(part * 2 * depth, 128) * 128, WIDTH - BLOCK)
            shape = (BLOCK, BLOCK)
            lane = within(iota(shape, 1), 128)
            column = over(iota(shape, 1), 128) * depth + lane + (part * 2 * depth - window)
            select = ((iota(shape, 0) == column) & (lane < depth)).astype(LOW)
            taken = dot(r.tall[:, pl.ds(pl.multiple_of(window, 128), BLOCK)], select)

            def beside(low, high):
                return [
                    low[:, one * 128 : (one + 1) * 128]
                    + pltpu.roll(high[:, one * 128 : (one + 1) * 128], depth, 1)
                    for one in range(2)
                ]

            for half in range(CORES):
                base = half * PAIR_ROWS // 2
                both = beside(taken[base : base + 48], taken[base + 48 : base + 96])
                for one in range(2):
                    at = half * CHIPS + 2 * part + one
                    target[at, first_row : first_row + 48, :] = act(
                        2 * part + one, both[one]
                    ).astype(LOW)
            if first_row:
                left = beside(taken[PAIR_ROWS : PAIR_ROWS + PAD], taken[PAIR_ROWS + PAD :])
                for half in range(CORES):
                    for one in range(2):
                        target[half * CHIPS + 2 * part + one, 0:PAD, :] = left[one].astype(LOW)

        return run

    def pack_coefs(coefs):
        shape = (PAIR_ROWS, GROUPS * 128)
        folds = over(iota(shape, 0), PAD) + over(iota(shape, 1), 128) * PAD == within(
            iota(shape, 1), 128
        )
        lanes = contract(coefs, folds.astype(LOW), 0, 0).astype(LOW)
        total = None
        for group in range(GROUPS):
            part = dot(r.slot_hot[group], lanes[:, group * 128 : (group + 1) * 128])
            total = part if total is None else total + part
        return total.astype(LOW).reshape(DEVICES, PAD, 128)


    def down_part(part):
        at = pl.ds(pl.multiple_of(part * BLOCK, BLOCK), BLOCK)
        r.wide_cls[:, at] = dot(r.active_cls[...], r.wc[:, at])

    every(0, WIDTH // BLOCK, down_part)
    down_pre = r.wide_cls[:, 0:WIDTH] + vector(5)
    normed_two, inverse_two = norm_parts(hidden_cls + down_pre)
    summary = normed_two * vector(6) + vector(7)
    magnitude = jnp.sqrt(jnp.sum(summary * summary, axis=-1, keepdims=True) + EPSILON)
    unit = jnp.where(real_row, summary / magnitude, 0.0)
    r.units[here] = unit.astype(LOW)

    steps_u[0]()
    r.tall[0:PAIR_ROWS, :] = dot(probs_low, r.embedded[...]).astype(LOW)
    r.tall[PAIR_ROWS : PAIR_ROWS + PAD, :] = context_cls
    r.tall[PAIR_ROWS + PAD :, :] = embedded_cls
    pack_one = pack_tall(r.mail_one, PAD, lambda at, both: both)

    def pack_one_step(part):
        pack_one(part)
        pl.when(part == 0)(steps_u[1])
        pl.when(part == 4)(steps_u[2])

    every(0, CHIPS // 2, pack_one_step)
    r.mail_one[:, 64:80, :] = pack_coefs(probs_low)
    steps_u[3]()

    def post_one(box, got, index, step):
        other, to_core, to_chip = peer(step)
        remote(
            box.at[other], got.at[me], r.one_send.at[index], r.one_recv.at[index], to_core, to_chip
        ).start()

    def post(box, got, index):
        every(1, DEVICES, partial(post_one, box, got, index))
        got[me] = box[me]


    r.got_one[me] = r.mail_one[me]

    def open_step(tile):
        open_tile(tile)
        pl.when(tile == 0)(steps_e[3])
        pl.when(tile == 2)(steps_u[4])

    def feed_step(steps, part):
        feed_up(part)
        for index in range(3):
            step = 3 * part + index + 1
            pl.when(step < DEVICES)(partial(post_one, r.mail_one, r.got_one, 1, step))
        for index, step in steps:
            pl.when(part == index)(step)

    first_parts, parts = 6, WIDE // BLOCK
    every(0, TOKENS // BLOCK, open_step)
    r.tile_up[...] = up_product(0)
    every(0, first_parts, partial(feed_step, [(1, steps_u[5]), (2, steps_e[4]), (5, steps_e[5])]))

    units = r.units[...].reshape(SLOT_ROWS, WIDTH)
    weight_row, pair_row, side_row = r.pairs[0:1, :], r.pairs[1:2, :], r.pairs[2:3, :]

    def pair_scores(rows, pair_col, side_col):
        opposite = side_col + side_row == 1.0
        partner = opposite & (pair_col == pair_row)
        raw = SCORE_SCALE * dot_turned(rows, units)
        shifted = jnp.where(partner, raw - SCORE_SCALE * MARGIN_WIDTH, raw)
        return jnp.where(opposite, shifted, MASK_FLOOR), partner

    every_score, every_partner = pair_scores(
        units, r.pairs_col[:, 1:2], r.pairs_col[:, 2:3]
    )
    peak_row = jnp.max(every_score, axis=0, keepdims=True)
    log_row = peak_row + jnp.log(
        jnp.sum(jnp.exp(every_score - peak_row), axis=0, keepdims=True)
    )
    picked_row = jnp.sum(jnp.where(every_partner, every_score, 0.0), axis=0, keepdims=True)
    r.loss[...] = jnp.sum(weight_row * (log_row - picked_row), axis=1, keepdims=True)

    rows_here = pl.ds(pl.multiple_of(me * PAD, 16), PAD)
    own_score, own_partner = pair_scores(
        r.units[here], r.pairs_col[rows_here, 1:2], r.pairs_col[rows_here, 2:3]
    )
    own_partner = own_partner.astype(FULL)
    own_peak = jnp.max(own_score, axis=1, keepdims=True)
    own_exp = jnp.exp(own_score - own_peak)
    own_share = own_exp / jnp.sum(own_exp, axis=1, keepdims=True)
    by_row = (r.pairs_col[rows_here, 0:1] * (own_share - own_partner)).astype(LOW)
    by_column = (weight_row * (jnp.exp(own_score - log_row) - own_partner)).astype(LOW)
    unit_grad = SCORE_SCALE * (dot(by_row, units) + dot(by_column, units))
    along = jnp.sum(unit * unit_grad, axis=-1, keepdims=True)
    summary_grad = (unit_grad - unit * along) / magnitude

    residual_grad, grad_g2, grad_s2 = norm_back_parts(
        summary_grad, normed_two, inverse_two, vector(6)
    )
    down_grad = residual_grad.astype(LOW)
    r.downs[here] = down_grad
    steps_d[0]()
    r.hidden_cls[...] = down_grad

    def up_back(part):
        at = pl.ds(pl.multiple_of(part * WIDTH, BLOCK), WIDTH)
        act_grad = dot_turned(r.hidden_cls[...], r.wc[at, :])
        r.active_cls[:, at] = (act_grad * r.slope_cls[:, at]).astype(LOW)

    every(0, WIDE // WIDTH, up_back)
    steps_d[1]()

    def hidden_back(part):
        at = pl.ds(pl.multiple_of(part * BLOCK, BLOCK), BLOCK)
        r.wide_cls[:, at] = dot_turned(r.active_cls[...], r.wb[at, :])

    every(0, WIDTH // BLOCK, hidden_back)
    hidden_grad = r.wide_cls[:, 0:WIDTH] + residual_grad
    first_grad, grad_g1, grad_s1 = norm_back_parts(
        hidden_grad, r.normed_one[...], inverse_one, vector(3)
    )
    attend_grad = first_grad.astype(LOW)
    context_grad = dot_turned(attend_grad, r.wa[:, 3 * WIDTH : 4 * WIDTH]).astype(LOW)
    attend_here = r.attends.at[here]
    attend_here[:, 0:WIDTH] = attend_grad
    attend_here[:, WIDTH : 2 * WIDTH] = context_grad
    steps_a[0]()
    steps_d[2]()
    context_tall = spread(context_grad)
    probs = r.probs[...]
    prob_grad = dot_turned(context_tall, r.qkv[:, values])
    inner = jnp.sum(probs * prob_grad, axis=1, keepdims=True)
    score_grad = (probs * (prob_grad - inner)).astype(LOW)
    steps_a[1]()
    r.mail_two[:, 48:64, :] = pack_coefs(score_grad)
    query_grad = (fold(dot(score_grad, r.qkv[:, keys])) * scale).astype(LOW)
    probs_total = jnp.sum(probs_low.astype(FULL), axis=1, keepdims=True)
    grad_bvalue = jnp.sum(probs_total * context_tall.astype(FULL), axis=0, keepdims=True)
    grad_bquery = jnp.sum(query_grad.astype(FULL), axis=0, keepdims=True)
    r.queries[here] = query_grad
    own_sums = jnp.concatenate(
        [jnp.zeros((2 * depth, WIDTH), FULL)]
        + [grad_bquery, grad_bvalue, grad_g1, grad_s1, grad_g2, grad_s2]
        + [jnp.zeros((128 - 2 * depth - 6, WIDTH), FULL)],
        axis=0,
    )
    r.own_sums[...] = jnp.transpose(own_sums)
    steps_q[0]()
    steps_a[2]()
    r.tall[0:PAIR_ROWS, :] = (dot(score_grad, r.embedded[...]) * scale).astype(LOW)

    def with_sums(at, both):
        return both + r.own_sums[pl.ds(pl.multiple_of(at * depth, 16), depth), :]

    every(0, CHIPS // 2, pack_tall(r.mail_two, 0, with_sums))
    steps_q[1]()
    post(r.mail_two, r.got_two, 2)

    def all_rows(buffer, start, width=WIDTH):
        return buffer[:, :, :, :, start : start + width].reshape(SLOT_ROWS, width)

    quarter_rows_count = quarter_size * PAD

    def from_sent(quarter):
        span = pl.ds(pl.multiple_of(quarter * quarter_rows_count, 128), quarter_rows_count)
        shape = (GROUPS * quarter_rows_count, quarter_rows_count)
        lanes = (iota(shape, 1) + quarter * quarter_rows_count).astype(FULL)
        named = r.found[0:GROUPS, span, 1:2].reshape(GROUPS * quarter_rows_count, 1)
        return (named == lanes).astype(LOW), span

    def quarter_part(buffer, quarter, start):
        planes = pl.ds(lax.rem(quarter, 2) * 2, 2)
        part = buffer[lax.div(quarter, 2), planes, :, :, start : start + BLOCK]
        return part.reshape(quarter_rows_count, BLOCK)

    def widened(coefs, group, start):
        lanes = iota((128, BLOCK), 0) == over(iota((128, BLOCK), 1) + start, HEAD) + group * PAD
        return dot(coefs, lanes.astype(LOW))

    half_wide = WIDE // 2

    def slope_tile(part):
        at = pl.ds(pl.multiple_of(core * half_wide + part * BLOCK, BLOCK), BLOCK)
        up_pre = dot(all_rows(r.early, 0), r.wb[:, at]) + r.up_bias[0:1, at]
        _, slope = gelu_parts(up_pre)
        r.slopes[:, pl.ds(pl.multiple_of(part * BLOCK, BLOCK), BLOCK)] = slope.astype(LOW)

    def slot_queries(quarter):
        sents, span = from_sent(quarter)
        for start in range(0, WIDTH, BLOCK):
            rows = dot(sents, quarter_part(r.early, quarter, WIDTH + start)).astype(LOW)
            rows = rows.reshape(GROUPS, quarter_rows_count, BLOCK)
            r.slot_query[:, span, start : start + BLOCK] = rows

    def activate():
        at = pl.ds(pl.multiple_of(chip // 2 * 2 * deep, 128), 2 * deep)
        up_pre = dot(all_rows(r.early, 0), r.wb[:, at]) + r.up_bias[0:1, at]
        r.active_turned[...] = jnp.transpose(gelu(up_pre)).astype(LOW)
        r.hidden_turned[...] = jnp.transpose(all_rows(r.early, 0))

    rest = [steps_d[3], steps_a[3], steps_q[2], steps_d[4], steps_a[4]]
    rest = [(first_parts + index, step) for index, step in enumerate(rest)]
    every(first_parts, parts - 1, partial(feed_step, rest))
    feed_up(parts - 1, last=True)

    def rest_step(part):
        feed_rest(part)
        for index, step in enumerate([steps_q[3], steps_d[5], steps_a[5]]):
            pl.when(part == index)(step)

    every(0, WIDTH // BLOCK, rest_step)
    steps_q[4]()
    every(0, WIDTH // BLOCK, feed_down)
    every(0, TOKENS // BLOCK, close_tile)
    every(0, 4, slot_queries)
    every(0, 6, slope_tile)
    activate()

    all_but_one(r.got_one, 1).wait_recv()
    def slot_probs(group):
        got_probs = r.got_one[:, 64:80, :].reshape(SLOT_ROWS, 128)
        for start in range(0, WIDTH, BLOCK):
            r.replies[group, :, start : start + BLOCK] = widened(got_probs, group, start).astype(LOW)

    def slot_values(quarter):
        sents, span = from_sent(quarter)
        for start in range(0, WIDTH, BLOCK):
            lanes = slice(start, start + BLOCK)
            rows = dot(sents, quarter_part(r.attends, quarter, WIDTH + start))
            rows = rows.reshape(GROUPS, quarter_rows_count, BLOCK)
            rows = r.replies[:, span, lanes].astype(FULL) * rows
            r.replies[:, span, lanes] = rows.astype(LOW)

    every(0, GROUPS, slot_probs)
    every(0, 4, slot_values)

    def head_products(got, first_row, right, start, target):
        def one_head(head):
            lane = core * (WIDTH // 2) + lax.div(head, 2) * 128
            pair_rows = right[:, :, :, :, pl.ds(pl.multiple_of(start + lane, 128), 128)]
            row = pl.ds(pl.multiple_of(first_row + lax.rem(head, 3) * PAD, 16), PAD)
            block_rows = got[:, row, :].reshape(SLOT_ROWS, 128)
            r.product[...] = contract(block_rows, pair_rows.reshape(SLOT_ROWS, 128), 0, 0)
            part = r.product[pl.ds(pl.multiple_of(lax.div(head, 3) * depth, 16), depth), :]
            at = pl.ds(pl.multiple_of(lane, 128), 128)
            own_lanes = over(iota((depth, 128), 1), HEAD) == lax.rem(head, 2)
            target[:, at] = jnp.where(own_lanes, part, target[:, at])

        every(0, HEADS // 2, one_head)

    def half_of(ref, at_core):
        half = ref.shape[1] // 2
        return ref.at[:, pl.ds(pl.multiple_of(at_core * half, 128), half)]

    def half_copy(index, ref, at_core):
        part = half_of(ref, at_core)
        return remote(part, part, r.half_send.at[index], r.half_recv.at[index], 1 - core, chip)

    own_half = pl.ds(pl.multiple_of(core * (WIDTH // 2), 128), WIDTH // 2)
    r.g_wv[:, own_half] = jnp.zeros((depth, WIDTH // 2), FULL)
    r.g_wk[:, own_half] = jnp.zeros((depth, WIDTH // 2), FULL)
    head_products(r.got_one, PAD, r.attends, WIDTH, r.g_wv)
    half_copy(0, r.g_wv, core).start()

    downs = r.downs[...].reshape(SLOT_ROWS, WIDTH)
    attends = all_rows(r.attends, 0)

    def up_tile(part):
        at = pl.ds(pl.multiple_of(core * half_wide + part * BLOCK, BLOCK), BLOCK)
        slope = r.slopes[:, pl.ds(pl.multiple_of(part * BLOCK, BLOCK), BLOCK)].astype(FULL)
        up_all = (dot_turned(r.downs[...].reshape(SLOT_ROWS, WIDTH), r.wc[at, :]) * slope)
        up_all = up_all.astype(LOW)
        r.g_wup[0:depth, at] = dot(r.hidden_turned[mine, :], up_all)
        total = jnp.sum(up_all.astype(FULL), axis=0, keepdims=True)
        r.g_wup[depth : depth + 8, at] = jnp.broadcast_to(total, (8, BLOCK))

    every(0, half_wide // BLOCK, up_tile)
    half_copy(1, r.g_wup, core).start()
    r.g_wdown[...] = dot(r.active_turned[pl.ds(pl.multiple_of(chip % 2 * deep, 16), deep), :], downs)
    r.left_turned[...] = jnp.transpose(r.got_one[:, 0:PAD, :].reshape(SLOT_ROWS, 128))
    r.g_wo[...] = dot(r.left_turned[0:depth, :], attends)
    own_lanes = (iota((WIDTH, 128), 0) == chip * depth + iota((WIDTH, 128), 1)).astype(LOW)

    def own_part(rows, select):
        total = None
        for _ in range(3):
            part = rows.astype(LOW)
            rows = rows - part.astype(FULL)
            picked = dot(part, select)
            total = picked if total is None else total + picked
        return total

    for quarter in range(4):
        rows_of(quarter).wait_send()
    all_but_one(r.got_two, 2).wait_recv()

    def slot_grads(group):
        got_scores = r.got_two[:, 48:64, :].reshape(SLOT_ROWS, 128)
        for start in range(0, WIDTH, BLOCK):
            lanes = slice(start, start + BLOCK)
            rows = r.slot_query[group, :, lanes].astype(FULL)
            rows = widened(got_scores, group, start) * rows * scale
            r.slot_query[group, :, lanes] = rows.astype(LOW)
        for start in range(0, WIDTH, BLOCK):
            lanes = slice(start, start + BLOCK)
            row_grad = dot_turned(r.slot_query[group], r.wa[lanes, keys])
            row_grad = row_grad + dot_turned(r.replies[group], r.wa[lanes, values])
            r.rows[group, :, lanes] = row_grad.astype(LOW)

    every(0, GROUPS, slot_grads)
    steps_q[5]()
    query_grads = all_rows(r.queries, 0)
    extra = dot_turned(query_grads, r.wa[:, 0:WIDTH]) + attends.astype(FULL)
    r.extra[...] = extra.astype(LOW)
    r.g_wq[...] = dot(r.left_turned[depth : 2 * depth, :], query_grads)

    half_rows = VOCAB_ROWS // 2

    def table_copy(tile):
        at = pl.ds(pl.multiple_of(tile * half_rows, BLOCK), half_rows)
        return pltpu.make_async_copy(
            r.table_full.at[at], r.table_grad.at[at], r.table_sem.at[tile]
        )

    def table_tile(tile):
        at = pl.ds(pl.multiple_of(tile * half_rows, BLOCK), half_rows)
        for start in range(0, WIDTH, BLOCK):
            lanes = slice(start, start + BLOCK)
            slot_rows = r.rows[:, :, lanes].reshape(GROUPS * SLOT_ROWS, BLOCK)
            r.table_full[at, lanes] = dot(r.by_row[at, 0 : GROUPS * SLOT_ROWS], slot_rows) + dot(
                r.by_row[at, GROUPS * SLOT_ROWS :], r.extra[:, lanes]
            )
        table_copy(tile).start()

    every(0, 2, table_tile)
    head_products(r.got_two, 0, r.early, WIDTH, r.g_wk)
    half_copy(2, r.g_wk, core).start()

    down_total = jnp.sum(downs.astype(FULL), axis=0, keepdims=True)
    attend_total = jnp.sum(attends.astype(FULL), axis=0, keepdims=True)
    sums = jnp.sum(r.got_two[:, 0:48, :].astype(FULL), axis=0)
    sums = jnp.concatenate([sums, jnp.zeros((128 - 48, 128), FULL)], axis=0)
    stacked = jnp.concatenate([attend_total, down_total, jnp.zeros((6, WIDTH), FULL)], axis=0)
    r.g_small[8:16, 0:128] = own_part(stacked, own_lanes)
    r.g_small[0:8, 0:128] = jnp.transpose(sums)[2 * depth : 2 * depth + 8, :]
    r.g_small[0:16, 128:BLOCK] = jnp.zeros((PAD, BLOCK - 128), FULL)
    half_copy(1, r.g_wup, 1 - core).wait_recv()
    up_lanes = (iota((WIDE, BLOCK), 0) == chip * deep + iota((WIDE, BLOCK), 1)).astype(LOW)
    r.g_small[16:24, :] = own_part(r.g_wup[depth : depth + 8, :], up_lanes)

    half_copy(0, r.g_wv, 1 - core).wait_recv()
    half_copy(2, r.g_wk, 1 - core).wait_recv()
    for index, ref in enumerate([r.g_wv, r.g_wup, r.g_wk]):
        half_copy(index, ref, core).wait_send()

    for index, ref in enumerate([r.every_ids, r.got_one, r.got_two]):
        all_but_one(ref, index).wait_send()
    all_smalls().wait_send()
    for end in [drain_a, drain_b, drain_c, drain_u, drain_e, drain_d, drain_a2, drain_q]:
        end()
    every(0, TOKENS // BLOCK, lambda tile: layer_copy(tile).wait())
    every(0, 2, lambda tile: table_copy(tile).wait())


def layer(inputs):
    dma = pltpu.SemaphoreType.DMA
    vmem = pl.BlockSpec(memory_space=pltpu.VMEM)
    anywhere = pl.BlockSpec(memory_space=pl.ANY)
    depth, deep = WIDTH // CHIPS, WIDE // CHIPS

    def gathered(width):
        return pltpu.VMEM((CORES, PLANES, LINES, PAD, width), LOW)

    outputs = dict(
        layer_out=((TOKENS, WIDTH), LOW),
        table_grad=((VOCAB_ROWS, WIDTH), FULL),
        g_wq=((depth, WIDTH), FULL),
        g_wk=((depth, WIDTH), FULL),
        g_wv=((depth, WIDTH), FULL),
        g_wo=((depth, WIDTH), FULL),
        g_wup=((depth + 8, WIDE), FULL),
        g_wdown=((deep, WIDTH), FULL),
        g_small=((24, BLOCK), FULL),
        loss=((1, 1), FULL),
    )
    scratch = dict(
        ids=pltpu.VMEM((8, 128), jnp.int32),
        every_ids=pltpu.VMEM((DEVICES, 8, 128), jnp.int32),
        rank=pltpu.VMEM((DEVICES, TOKENS), FULL),
        code=pltpu.VMEM((DEVICES, TOKENS), FULL),
        found=pltpu.VMEM((GROUPS + 1, SLOT_ROWS, 2), FULL),
        block_bias=pltpu.VMEM((2 * BLOCK, BLOCK // 2), FULL),
        valid_bias=pltpu.VMEM((8, TOKENS), FULL),
        slot_col=pltpu.VMEM((TOKENS, 1), FULL),
        slot_line=pltpu.VMEM((8, TOKENS), FULL),
        valid_col=pltpu.VMEM((TOKENS, 1), FULL),
        valid_line=pltpu.VMEM((8, TOKENS), FULL),
        pairs=pltpu.VMEM((8, SLOT_ROWS), FULL),
        pairs_col=pltpu.VMEM((SLOT_ROWS, 128), FULL),
        vectors=pltpu.VMEM((PAD, WIDTH), FULL),
        up_bias=pltpu.VMEM((8, WIDE), FULL),
        qkv_bias=pltpu.VMEM((8, 3 * WIDTH), FULL),
        smalls=pltpu.VMEM((PAD, CHIPS * 128), LOW),
        wa=pltpu.VMEM((WIDTH, 4 * WIDTH), LOW),
        wb=pltpu.VMEM((WIDTH, WIDE), LOW),
        wc=pltpu.VMEM((WIDE, WIDTH), LOW),
        chosen=pltpu.VMEM((GROUPS, SLOT_ROWS, VOCAB_ROWS), LOW),
        by_row=pltpu.VMEM((VOCAB_ROWS, (GROUPS + 1) * SLOT_ROWS), LOW),
        rows=pltpu.VMEM((GROUPS, SLOT_ROWS, WIDTH), LOW),
        replies=pltpu.VMEM((GROUPS, SLOT_ROWS, WIDTH), LOW),
        slot_query=pltpu.VMEM((GROUPS, SLOT_ROWS, WIDTH), LOW),
        extra=pltpu.VMEM((SLOT_ROWS, WIDTH), LOW),
        hidden_cls=pltpu.VMEM((PAD, WIDTH), LOW),
        active_cls=pltpu.VMEM((PAD, WIDE), LOW),
        slope_cls=pltpu.VMEM((PAD, WIDE), FULL),
        wide_cls=pltpu.VMEM((PAD, WIDTH), FULL),
        tall=pltpu.VMEM((PAIR_ROWS + 2 * PAD, WIDTH), LOW),
        own_sums=pltpu.VMEM((WIDTH, 128), FULL),
        product=pltpu.VMEM((128, 128), FULL),
        slot_hot=pltpu.VMEM((GROUPS, SLOT_ROWS, TOKENS), LOW),
        tile_up=pltpu.VMEM((TOKENS, BLOCK), FULL),
        embedded=pltpu.VMEM((TOKENS, WIDTH), LOW),
        qkv=pltpu.VMEM((TOKENS, 3 * WIDTH), LOW),
        context=pltpu.VMEM((TOKENS, WIDTH), LOW),
        table_full=pltpu.VMEM((VOCAB_ROWS, WIDTH), FULL),
        probs=pltpu.VMEM((PAIR_ROWS, TOKENS), FULL),
        normed_one=pltpu.VMEM((PAD, WIDTH), FULL),
        units=gathered(WIDTH),
        early=gathered(2 * WIDTH),
        downs=gathered(WIDTH),
        attends=gathered(2 * WIDTH),
        queries=gathered(WIDTH),
        slopes=pltpu.VMEM((SLOT_ROWS, WIDE // 2), LOW),
        hidden_turned=pltpu.VMEM((WIDTH, SLOT_ROWS), LOW),
        active_turned=pltpu.VMEM((2 * deep, SLOT_ROWS), LOW),
        left_turned=pltpu.VMEM((128, SLOT_ROWS), LOW),
        mail_one=pltpu.VMEM((DEVICES, 80, 128), LOW),
        got_one=pltpu.VMEM((DEVICES, 80, 128), LOW),
        mail_two=pltpu.VMEM((DEVICES, 64, 128), LOW),
        got_two=pltpu.VMEM((DEVICES, 64, 128), LOW),
        rows_send=dma((4,)),
        rows_recv=dma((4,)),
        one_send=dma((4,)),
        one_recv=dma((4,)),
        small_send=dma((1,)),
        small_recv=dma((1,)),
        weight_send=dma((3, 7)),
        weight_recv=dma((3, 18)),
        gather_send=dma((5, 13)),
        gather_recv=dma((5, 13)),
        half_send=dma((3,)),
        half_recv=dma((3,)),
        out_sem=dma((TOKENS // BLOCK,)),
        table_sem=dma((2,)),
    )
    names = INPUTS + OUTPUTS + list(scratch)
    return pl.pallas_call(
        partial(layer_kernel, names),
        out_shape=tuple(jax.ShapeDtypeStruct(*outputs[name]) for name in OUTPUTS),
        in_specs=[vmem] * len(INPUTS),
        out_specs=(anywhere, anywhere) + (vmem,) * (len(OUTPUTS) - 2),
        scratch_shapes=list(scratch.values()),
        compiler_params=pltpu.CompilerParams(
            collective_id=0, has_side_effects=True, vmem_limit_bytes=VMEM_LIMIT
        ),
        name="layer",
    )(*inputs)


def finish_kernel(count, *refs):
    large, (small, loss), outs = refs[:count], refs[count : count + 2], refs[count + 2 : -1]
    sems = refs[-1]
    copies = []
    for index, (source, target) in enumerate(zip(large, outs)):
        part = source if source.shape == target.shape else source.at[: target.shape[0]]
        copies.append(pltpu.make_async_copy(part, target, sems.at[index]))
        copies[-1].start()
    for row, target in zip([0, 1, 8, 2, 3, 16, 9, 4, 5], outs[count : count + 9]):
        size = target.shape[0]
        target[...] = small[row : row + 1, 0:size].reshape(size)
    outs[-1][...] = loss[...].reshape(1)
    for one in copies:
        one.wait()


def finish(results):
    vmem = pl.BlockSpec(memory_space=pltpu.VMEM)
    anywhere = pl.BlockSpec(memory_space=pl.ANY)
    depth, deep = WIDTH // CHIPS, WIDE // CHIPS
    count = len(results) - 2
    shapes = [(one.shape, one.dtype) for one in results[:count]]
    shapes[6] = ((depth, WIDE), FULL)
    shapes += [((depth,), FULL)] * 5 + [((deep,), FULL)] + [((depth,), FULL)] * 3
    shapes.append(((1,), FULL))
    return pl.pallas_call(
        partial(finish_kernel, count),
        out_shape=tuple(jax.ShapeDtypeStruct(*one) for one in shapes),
        in_specs=[vmem] * (count + 2),
        out_specs=(anywhere,) * count + (vmem,) * 10,
        scratch_shapes=[pltpu.SemaphoreType.DMA((count,))],
        name="finish",
    )(*results)


def block_body(
    table,
    token_ids,
    sent_lengths,
    pair_slot,
    pair_lang,
    *parameters,
):
    results = finish(layer((table, token_ids, sent_lengths, pair_slot, pair_lang) + parameters))
    layer_out, table_grad, g_wq, g_wk, g_wv, g_wo, g_wup, g_wdown = results[:8]
    g_bq, g_bv, g_bo, g_g1, g_s1, g_bup, g_bdown, g_g2, g_s2, loss = results[8:]
    return (
        layer_out.reshape(token_ids.shape + (WIDTH,)),
        loss.reshape(()),
        table_grad,
        g_wq,
        g_bq,
        g_wk,
        g_wv,
        g_bv,
        g_wo,
        g_bo,
        g_g1,
        g_s1,
        g_wup,
        g_bup,
        g_wdown,
        g_bdown,
        g_g2,
        g_s2,
    )


def solution(mesh):
    in_specs = (
        P(("dp", "fsdp"), None),
        P(("dp", "fsdp"), None),
        P(("dp", "fsdp")),
        P(),
        P(),
        P("fsdp", None),
        P("fsdp"),
        P("fsdp", None),
        P("fsdp", None),
        P("fsdp"),
        P("fsdp", None),
        P("fsdp"),
        P("fsdp"),
        P("fsdp"),
        P("fsdp", None),
        P("fsdp"),
        P("fsdp", None),
        P("fsdp"),
        P("fsdp"),
        P("fsdp"),
    )
    out_specs = (
        P(("dp", "fsdp"), None, None),
        P(),
        P(("dp", "fsdp"), None),
        P("fsdp", None),
        P("fsdp"),
        P("fsdp", None),
        P("fsdp", None),
        P("fsdp"),
        P("fsdp", None),
        P("fsdp"),
        P("fsdp"),
        P("fsdp"),
        P("fsdp", None),
        P("fsdp"),
        P("fsdp", None),
        P("fsdp"),
        P("fsdp"),
        P("fsdp"),
    )
    sizes = dict(mesh.shape)
    body = general_body
    if sizes["dp"] == CORES and sizes["fsdp"] == CHIPS:
        body = block_body
    return jax.shard_map(body, mesh=mesh, in_specs=in_specs, out_specs=out_specs, check_vma=False)
```

profile of v0, /device:TPU:0, one launch (start us, length us, event | category | flops | bytes accessed | tf_op | source)
XLA Modules:
  0.0 220.8 jit_solution(8330592350795046241)
XLA Ops:
  0.7 213.3 %layer.1 = (bf16[768,768]{1,0:T(8,128)(2,1)}, f32[1024,768]{1,0:T(8,128)}, f32[48,768]{1,0:T(8,128)}, f32[48,768]{1,0:T(8,128)}, f32[48,768]{1,0:T(8,128)}, /*in...) custom-call(bf16[1024,768]{1,0:T(8,128)(2,1)} %refs_0_.1, ...), custom_call_target="tpu_custom_call" | custom-call | tf_op jit(solution)/shard_map/layer/pallas_call | solution.py:1663
  214.0 6.6 %finish.1 = (bf16[768,768]{1,0:T(8,128)(2,1)}, f32[1024,768]{1,0:T(8,128)}, f32[48,768]{1,0:T(8,128)}, f32[48,768]{1,0:T(8,128)}, f32[48,768]{1,0:T(8,128)}, /*i...) custom-call(bf16[768,768]{1,0:T(8,128)(2,1)} %get-tuple-element.46.r, ...), custom_call_target="tpu_custom_call" | custom-call | tf_op jit(solution)/shard_map/finish/pallas_call | solution.py:1701
where the time goes:
time: 221 us
  Pallas kernels  220 us (100%)
    pallas_call x1, Pallas kernels, layer(): pl.pallas_call(partial(layer_kernel, names), out_shape=tuple((jax.ShapeDt...  213 us
    pallas_call x1, Pallas kernels, finish(): pl.pallas_call(partial(finish_kernel, count), out_shape=tuple((jax.ShapeD...  6.64 us

commit v1 on v0

--- a/solution.py
+++ b/solution.py
@@ -1154,13 +1154,14 @@
     every(0, WIDE // WIDTH, up_part)
     steps_e[1]()
 
-    def attend_step(unit):
-        attend(unit)
-        pl.when(unit == 1)(partial(move, (moves_c, 8)))
-        pl.when(unit == 3)(moves_c[10])
-        pl.when(unit == 4)(steps_e[2])
-
-    every(0, 6, attend_step)
+    def attend_step(pair):
+        attend(2 * pair)
+        attend(2 * pair + 1)
+        pl.when(pair == 0)(partial(move, (moves_c, 8)))
+        pl.when(pair == 1)(moves_c[10])
+        pl.when(pair == 2)(steps_e[2])
+
+    every(0, 3, attend_step)
     finish_c()
 
     def pack_tall(target, first_row, act):
@@ -1196,10 +1197,11 @@
         return run
 
     def pack_coefs(coefs):
-        shape = (PAIR_ROWS, GROUPS * 128)
-        folds = over(iota(shape, 0), PAD) + over(iota(shape, 1), 128) * PAD == within(
-            iota(shape, 1), 128
-        )
+        shape = (2 * PAIR_ROWS, GROUPS * 128)
+        row, lane = iota(shape, 0), iota(shape, 1)
+        kind = jnp.where(row >= PAIR_ROWS, PAD, 0)
+        head = over(row, PAD) - jnp.where(row >= PAIR_ROWS, HEADS, 0)
+        folds = head + kind + over(lane, 128) * 2 * PAD == within(lane, 128)
         lanes = contract(coefs, folds.astype(LOW), 0, 0).astype(LOW)
         total = None
         for group in range(GROUPS):
@@ -1226,13 +1228,13 @@
     r.tall[PAIR_ROWS + PAD :, :] = embedded_cls
     pack_one = pack_tall(r.mail_one, PAD, lambda at, both: both)
 
-    def pack_one_step(part):
-        pack_one(part)
-        pl.when(part == 0)(steps_u[1])
-        pl.when(part == 4)(steps_u[2])
-
-    every(0, CHIPS // 2, pack_one_step)
-    r.mail_one[:, 64:80, :] = pack_coefs(probs_low)
+    def pack_one_step(pair):
+        pack_one(2 * pair)
+        pack_one(2 * pair + 1)
+        pl.when(pair == 0)(steps_u[1])
+        pl.when(pair == 2)(steps_u[2])
+
+    every(0, CHIPS // 4, pack_one_step)
     steps_u[3]()
 
     def post_one(box, got, index, step):
@@ -1240,11 +1242,6 @@
         remote(
             box.at[other], got.at[me], r.one_send.at[index], r.one_recv.at[index], to_core, to_chip
         ).start()
-
-    def post(box, got, index):
-        every(1, DEVICES, partial(post_one, box, got, index))
-        got[me] = box[me]
-
 
     r.got_one[me] = r.mail_one[me]
 
@@ -1338,7 +1335,8 @@
     inner = jnp.sum(probs * prob_grad, axis=1, keepdims=True)
     score_grad = (probs * (prob_grad - inner)).astype(LOW)
     steps_a[1]()
-    r.mail_two[:, 48:64, :] = pack_coefs(score_grad)
+    r.mail_two[:, 48:64, :] = pack_coefs(jnp.concatenate([probs_low, score_grad], axis=0))
+    r.got_two[me, 48:64, :] = r.mail_two[me, 48:64, :]
     query_grad = (fold(dot(score_grad, r.qkv[:, keys])) * scale).astype(LOW)
     probs_total = jnp.sum(probs_low.astype(FULL), axis=1, keepdims=True)
     grad_bvalue = jnp.sum(probs_total * context_tall.astype(FULL), axis=0, keepdims=True)
@@ -1358,9 +1356,30 @@
     def with_sums(at, both):
         return both + r.own_sums[pl.ds(pl.multiple_of(at * depth, 16), depth), :]
 
-    every(0, CHIPS // 2, pack_tall(r.mail_two, 0, with_sums))
+    pack_two = pack_tall(r.mail_two, 0, with_sums)
+
+    def send_two(at):
+        remote(
+            r.mail_two.at[at],
+            r.got_two.at[me],
+            r.one_send.at[2],
+            r.one_recv.at[2],
+            lax.div(at, CHIPS),
+            lax.rem(at, CHIPS),
+        ).start()
+
+    def pack_two_step(step):
+        pair = lax.rem(step + lax.div(chip, 4), CHIPS // 4)
+        pack_two(2 * pair)
+        pack_two(2 * pair + 1)
+        for half in range(CORES):
+            for one in range(4):
+                at = half * CHIPS + 4 * pair + one
+                pl.when(at != me)(partial(send_two, at))
+
+    every(0, CHIPS // 4, pack_two_step)
+    r.got_two[me, 0:48, :] = r.mail_two[me, 0:48, :]
     steps_q[1]()
-    post(r.mail_two, r.got_two, 2)
 
     def all_rows(buffer, start, width=WIDTH):
         return buffer[:, :, :, :, start : start + width].reshape(SLOT_ROWS, width)
@@ -1379,8 +1398,9 @@
         part = buffer[lax.div(quarter, 2), planes, :, :, start : start + BLOCK]
         return part.reshape(quarter_rows_count, BLOCK)
 
-    def widened(coefs, group, start):
-        lanes = iota((128, BLOCK), 0) == over(iota((128, BLOCK), 1) + start, HEAD) + group * PAD
+    def widened(coefs, group, start, kind):
+        lane_head = over(iota((128, BLOCK), 1) + start, HEAD)
+        lanes = iota((128, BLOCK), 0) == lane_head + group * 2 * PAD + kind
         return dot(coefs, lanes.astype(LOW))
 
     half_wide = WIDE // 2
@@ -1416,17 +1436,30 @@
 
     every(0, WIDTH // BLOCK, rest_step)
     steps_q[4]()
-    every(0, WIDTH // BLOCK, feed_down)
+
+    def down_step(part):
+        feed_down(part)
+        for index, ends in enumerate([[drain_a, drain_b], [drain_c, drain_u], [drain_e]]):
+            for end in ends:
+                pl.when(part == index)(end)
+
+    every(0, WIDTH // BLOCK, down_step)
     every(0, TOKENS // BLOCK, close_tile)
     every(0, 4, slot_queries)
-    every(0, 6, slope_tile)
+
+    def slope_two(pair):
+        slope_tile(2 * pair)
+        slope_tile(2 * pair + 1)
+
+    every(0, 3, slope_two)
     activate()
 
     all_but_one(r.got_one, 1).wait_recv()
+    all_but_one(r.got_two, 2).wait_recv()
     def slot_probs(group):
-        got_probs = r.got_one[:, 64:80, :].reshape(SLOT_ROWS, 128)
+        got = r.got_two[:, 48:64, :].reshape(SLOT_ROWS, 128)
         for start in range(0, WIDTH, BLOCK):
-            r.replies[group, :, start : start + BLOCK] = widened(got_probs, group, start).astype(LOW)
+            r.replies[group, :, start : start + BLOCK] = widened(got, group, start, 0).astype(LOW)
 
     def slot_values(quarter):
         sents, span = from_sent(quarter)
@@ -1485,27 +1518,22 @@
     r.g_wdown[...] = dot(r.active_turned[pl.ds(pl.multiple_of(chip % 2 * deep, 16), deep), :], downs)
     r.left_turned[...] = jnp.transpose(r.got_one[:, 0:PAD, :].reshape(SLOT_ROWS, 128))
     r.g_wo[...] = dot(r.left_turned[0:depth, :], attends)
-    own_lanes = (iota((WIDTH, 128), 0) == chip * depth + iota((WIDTH, 128), 1)).astype(LOW)
-
-    def own_part(rows, select):
-        total = None
-        for _ in range(3):
-            part = rows.astype(LOW)
-            rows = rows - part.astype(FULL)
-            picked = dot(part, select)
-            total = picked if total is None else total + picked
-        return total
+
+    def own_part(rows, size):
+        start = chip * size
+        window = jnp.minimum(lax.div(start, 128) * 128, rows.shape[1] - BLOCK)
+        part = rows[:, pl.ds(pl.multiple_of(window, 128), BLOCK)]
+        return pltpu.roll(part, lax.rem(BLOCK + window - start, BLOCK), 1)
 
     for quarter in range(4):
         rows_of(quarter).wait_send()
-    all_but_one(r.got_two, 2).wait_recv()
 
     def slot_grads(group):
         got_scores = r.got_two[:, 48:64, :].reshape(SLOT_ROWS, 128)
         for start in range(0, WIDTH, BLOCK):
             lanes = slice(start, start + BLOCK)
             rows = r.slot_query[group, :, lanes].astype(FULL)
-            rows = widened(got_scores, group, start) * rows * scale
+            rows = widened(got_scores, group, start, PAD) * rows * scale
             r.slot_query[group, :, lanes] = rows.astype(LOW)
         for start in range(0, WIDTH, BLOCK):
             lanes = slice(start, start + BLOCK)
@@ -1546,13 +1574,12 @@
     attend_total = jnp.sum(attends.astype(FULL), axis=0, keepdims=True)
     sums = jnp.sum(r.got_two[:, 0:48, :].astype(FULL), axis=0)
     sums = jnp.concatenate([sums, jnp.zeros((128 - 48, 128), FULL)], axis=0)
-    stacked = jnp.concatenate([attend_total, down_total, jnp.zeros((6, WIDTH), FULL)], axis=0)
-    r.g_small[8:16, 0:128] = own_part(stacked, own_lanes)
+    r.totals[...] = jnp.concatenate([attend_total, down_total, jnp.zeros((6, WIDTH), FULL)], axis=0)
+    r.g_small[8:16, :] = own_part(r.totals, depth)
     r.g_small[0:8, 0:128] = jnp.transpose(sums)[2 * depth : 2 * depth + 8, :]
-    r.g_small[0:16, 128:BLOCK] = jnp.zeros((PAD, BLOCK - 128), FULL)
+    r.g_small[0:8, 128:BLOCK] = jnp.zeros((8, BLOCK - 128), FULL)
     half_copy(1, r.g_wup, 1 - core).wait_recv()
-    up_lanes = (iota((WIDE, BLOCK), 0) == chip * deep + iota((WIDE, BLOCK), 1)).astype(LOW)
-    r.g_small[16:24, :] = own_part(r.g_wup[depth : depth + 8, :], up_lanes)
+    r.g_small[16:24, :] = own_part(r.g_wup.at[depth : depth + 8, :], deep)
 
     half_copy(0, r.g_wv, 1 - core).wait_recv()
     half_copy(2, r.g_wk, 1 - core).wait_recv()
@@ -1562,7 +1589,7 @@
     for index, ref in enumerate([r.every_ids, r.got_one, r.got_two]):
         all_but_one(ref, index).wait_send()
     all_smalls().wait_send()
-    for end in [drain_a, drain_b, drain_c, drain_u, drain_e, drain_d, drain_a2, drain_q]:
+    for end in [drain_d, drain_a2, drain_q]:
         end()
     every(0, TOKENS // BLOCK, lambda tile: layer_copy(tile).wait())
     every(0, 2, lambda tile: table_copy(tile).wait())
@@ -1640,8 +1667,9 @@
         hidden_turned=pltpu.VMEM((WIDTH, SLOT_ROWS), LOW),
         active_turned=pltpu.VMEM((2 * deep, SLOT_ROWS), LOW),
         left_turned=pltpu.VMEM((128, SLOT_ROWS), LOW),
-        mail_one=pltpu.VMEM((DEVICES, 80, 128), LOW),
-        got_one=pltpu.VMEM((DEVICES, 80, 128), LOW),
+        totals=pltpu.VMEM((8, WIDTH), FULL),
+        mail_one=pltpu.VMEM((DEVICES, 64, 128), LOW),
+        got_one=pltpu.VMEM((DEVICES, 64, 128), LOW),
         mail_two=pltpu.VMEM((DEVICES, 64, 128), LOW),
         got_two=pltpu.VMEM((DEVICES, 64, 128), LOW),
         rows_send=dma((4,)),

time: 221 us -> 225 us (1.018)
  Pallas kernels: 220 us -> 224 us
    pallas_call x1, Pallas kernels: 213 us -> 217 us  [layer(): pl.pallas_call(partial(layer_kernel, names), out_shape=tuple((jax.ShapeDt...]
where the time goes in v1:
time: 225 us; the launch traced here: 224 us
  Pallas kernels  224 us (100%)
    pallas_call x1, Pallas kernels, layer(): pl.pallas_call(partial(layer_kernel, names), out_shape=tuple((jax.ShapeDt...  217 us
    pallas_call x1, Pallas kernels, finish(): pl.pallas_call(partial(finish_kernel, count), out_shape=tuple((jax.ShapeD...  6.64 us

profile of v1, /device:TPU:0, one launch (start us, length us, event | category | flops | bytes accessed | tf_op | source)
XLA Modules:
  0.0 224.5 jit_solution(17406669026481948744)
XLA Ops:
  0.7 217.0 %layer.1 = (bf16[768,768]{1,0:T(8,128)(2,1)}, f32[1024,768]{1,0:T(8,128)}, f32[48,768]{1,0:T(8,128)}, f32[48,768]{1,0:T(8,128)}, f32[48,768]{1,0:T(8,128)}, /*in...) custom-call(bf16[1024,768]{1,0:T(8,128)(2,1)} %refs_0_.1, ...), custom_call_target="tpu_custom_call" | custom-call | tf_op jit(solution)/shard_map/layer/pallas_call | solution.py:1691
  217.7 6.6 %finish.1 = (bf16[768,768]{1,0:T(8,128)(2,1)}, f32[1024,768]{1,0:T(8,128)}, f32[48,768]{1,0:T(8,128)}, f32[48,768]{1,0:T(8,128)}, f32[48,768]{1,0:T(8,128)}, /*i...) custom-call(bf16[768,768]{1,0:T(8,128)(2,1)} %get-tuple-element.46.r, ...), custom_call_target="tpu_custom_call" | custom-call | tf_op jit(solution)/shard_map/finish/pallas_call | solution.py:1729

commit v2 on v1

--- a/solution.py
+++ b/solution.py
@@ -1082,15 +1082,15 @@
                 axis=0,
             )
             scores = dot_turned(stacked, key) + bias
-            shifted = jnp.exp(scores - jnp.max(scores, axis=1, keepdims=True))
-            probs = shifted * (1.0 / jnp.sum(shifted, axis=1, keepdims=True))
-            mixed = dot(probs.astype(LOW), value)
-            result = mixed[0:half_block]
+            shifted = jnp.exp(scores - jnp.max(scores, axis=1, keepdims=True)).astype(LOW)
+            mixed = dot(shifted, value)
+            totals = dot(shifted, jnp.ones((half_block, BLOCK), LOW))
+            result, total = mixed[0:half_block], totals[0:half_block]
             for head in range(1, 4):
-                result = jnp.where(
-                    lane_head == head, mixed[head * half_block : (head + 1) * half_block], result
-                )
-            r.context[rows, lane : lane + BLOCK] = result.astype(LOW)
+                at = slice(head * half_block, (head + 1) * half_block)
+                result = jnp.where(lane_head == head, mixed[at], result)
+                total = jnp.where(lane_head == head, totals[at], total)
+            r.context[rows, lane : lane + BLOCK] = (result / total).astype(LOW)
 
     def open_tile(tile):
         at = pl.ds(pl.multiple_of(tile * BLOCK, BLOCK), BLOCK)
@@ -1154,14 +1154,13 @@
     every(0, WIDE // WIDTH, up_part)
     steps_e[1]()
 
-    def attend_step(pair):
-        attend(2 * pair)
-        attend(2 * pair + 1)
-        pl.when(pair == 0)(partial(move, (moves_c, 8)))
-        pl.when(pair == 1)(moves_c[10])
-        pl.when(pair == 2)(steps_e[2])
-
-    every(0, 3, attend_step)
+    def attend_step(unit):
+        attend(unit)
+        pl.when(unit == 1)(partial(move, (moves_c, 8)))
+        pl.when(unit == 3)(moves_c[10])
+        pl.when(unit == 4)(steps_e[2])
+
+    every(0, 6, attend_step)
     finish_c()
 
     def pack_tall(target, first_row, act):
@@ -1228,13 +1227,12 @@
     r.tall[PAIR_ROWS + PAD :, :] = embedded_cls
     pack_one = pack_tall(r.mail_one, PAD, lambda at, both: both)
 
-    def pack_one_step(pair):
-        pack_one(2 * pair)
-        pack_one(2 * pair + 1)
-        pl.when(pair == 0)(steps_u[1])
-        pl.when(pair == 2)(steps_u[2])
-
-    every(0, CHIPS // 4, pack_one_step)
+    def pack_one_step(part):
+        pack_one(part)
+        pl.when(part == 0)(steps_u[1])
+        pl.when(part == 4)(steps_u[2])
+
+    every(0, CHIPS // 2, pack_one_step)
     steps_u[3]()
 
     def post_one(box, got, index, step):
@@ -1369,15 +1367,14 @@
         ).start()
 
     def pack_two_step(step):
-        pair = lax.rem(step + lax.div(chip, 4), CHIPS // 4)
-        pack_two(2 * pair)
-        pack_two(2 * pair + 1)
+        part = lax.rem(step + lax.div(chip, 2), CHIPS // 2)
+        pack_two(part)
         for half in range(CORES):
-            for one in range(4):
-                at = half * CHIPS + 4 * pair + one
+            for one in range(2):
+                at = half * CHIPS + 2 * part + one
                 pl.when(at != me)(partial(send_two, at))
 
-    every(0, CHIPS // 4, pack_two_step)
+    every(0, CHIPS // 2, pack_two_step)
     r.got_two[me, 0:48, :] = r.mail_two[me, 0:48, :]
     steps_q[1]()
 
@@ -1446,12 +1443,7 @@
     every(0, WIDTH // BLOCK, down_step)
     every(0, TOKENS // BLOCK, close_tile)
     every(0, 4, slot_queries)
-
-    def slope_two(pair):
-        slope_tile(2 * pair)
-        slope_tile(2 * pair + 1)
-
-    every(0, 3, slope_two)
+    every(0, 6, slope_tile)
     activate()
 
     all_but_one(r.got_one, 1).wait_recv()

time: 225 us -> 226 us (level)
  no operation moved by 1% of the time
where the time goes in v2:
time: 226 us; the launch traced here: 225 us
  Pallas kernels  225 us (100%)
    pallas_call x1, Pallas kernels, layer(): pl.pallas_call(partial(layer_kernel, names), out_shape=tuple((jax.ShapeDt...  218 us
    pallas_call x1, Pallas kernels, finish(): pl.pallas_call(partial(finish_kernel, count), out_shape=tuple((jax.ShapeD...  6.64 us

profile of v2, /device:TPU:0, one launch (start us, length us, event | category | flops | bytes accessed | tf_op | source)
XLA Modules:
  0.0 225.4 jit_solution(7815799709879424017)
XLA Ops:
  0.7 217.9 %layer.1 = (bf16[768,768]{1,0:T(8,128)(2,1)}, f32[1024,768]{1,0:T(8,128)}, f32[48,768]{1,0:T(8,128)}, f32[48,768]{1,0:T(8,128)}, f32[48,768]{1,0:T(8,128)}, /*in...) custom-call(bf16[1024,768]{1,0:T(8,128)(2,1)} %refs_0_.1, ...), custom_call_target="tpu_custom_call" | custom-call | tf_op jit(solution)/shard_map/layer/pallas_call | solution.py:1683
  218.6 6.6 %finish.1 = (bf16[768,768]{1,0:T(8,128)(2,1)}, f32[1024,768]{1,0:T(8,128)}, f32[48,768]{1,0:T(8,128)}, f32[48,768]{1,0:T(8,128)}, f32[48,768]{1,0:T(8,128)}, /*i...) custom-call(bf16[768,768]{1,0:T(8,128)(2,1)} %get-tuple-element.46.r, ...), custom_call_target="tpu_custom_call" | custom-call | tf_op jit(solution)/shard_map/finish/pallas_call | solution.py:1721

commit v3 on v2

--- a/solution.py
+++ b/solution.py
@@ -1082,15 +1082,15 @@
                 axis=0,
             )
             scores = dot_turned(stacked, key) + bias
-            shifted = jnp.exp(scores - jnp.max(scores, axis=1, keepdims=True)).astype(LOW)
-            mixed = dot(shifted, value)
-            totals = dot(shifted, jnp.ones((half_block, BLOCK), LOW))
-            result, total = mixed[0:half_block], totals[0:half_block]
+            shifted = jnp.exp(scores - jnp.max(scores, axis=1, keepdims=True))
+            probs = shifted * (1.0 / jnp.sum(shifted, axis=1, keepdims=True))
+            mixed = dot(probs.astype(LOW), value)
+            result = mixed[0:half_block]
             for head in range(1, 4):
-                at = slice(head * half_block, (head + 1) * half_block)
-                result = jnp.where(lane_head == head, mixed[at], result)
-                total = jnp.where(lane_head == head, totals[at], total)
-            r.context[rows, lane : lane + BLOCK] = (result / total).astype(LOW)
+                result = jnp.where(
+                    lane_head == head, mixed[head * half_block : (head + 1) * half_block], result
+                )
+            r.context[rows, lane : lane + BLOCK] = result.astype(LOW)
 
     def open_tile(tile):
         at = pl.ds(pl.multiple_of(tile * BLOCK, BLOCK), BLOCK)
@@ -1250,8 +1250,8 @@
 
     def feed_step(steps, part):
         feed_up(part)
-        for index in range(3):
-            step = 3 * part + index + 1
+        for index in range(6):
+            step = 6 * part + index + 1
             pl.when(step < DEVICES)(partial(post_one, r.mail_one, r.got_one, 1, step))
         for index, step in steps:
             pl.when(part == index)(step)
@@ -1367,12 +1367,12 @@
         ).start()
 
     def pack_two_step(step):
-        part = lax.rem(step + lax.div(chip, 2), CHIPS // 2)
+        part = lax.rem(step + lax.div(me, 4), CHIPS // 2)
         pack_two(part)
-        for half in range(CORES):
-            for one in range(2):
-                at = half * CHIPS + 2 * part + one
-                pl.when(at != me)(partial(send_two, at))
+        for index in range(4):
+            turn = lax.rem(index + me, 4)
+            at = lax.div(turn, 2) * CHIPS + 2 * part + lax.rem(turn, 2)
+            pl.when(at != me)(partial(send_two, at))
 
     every(0, CHIPS // 2, pack_two_step)
     r.got_two[me, 0:48, :] = r.mail_two[me, 0:48, :]
@@ -1447,7 +1447,6 @@
     activate()
 
     all_but_one(r.got_one, 1).wait_recv()
-    all_but_one(r.got_two, 2).wait_recv()
     def slot_probs(group):
         got = r.got_two[:, 48:64, :].reshape(SLOT_ROWS, 128)
         for start in range(0, WIDTH, BLOCK):
@@ -1461,9 +1460,6 @@
             rows = rows.reshape(GROUPS, quarter_rows_count, BLOCK)
             rows = r.replies[:, span, lanes].astype(FULL) * rows
             r.replies[:, span, lanes] = rows.astype(LOW)
-
-    every(0, GROUPS, slot_probs)
-    every(0, 4, slot_values)
 
     def head_products(got, first_row, right, start, target):
         def one_head(head):
@@ -1519,6 +1515,9 @@
 
     for quarter in range(4):
         rows_of(quarter).wait_send()
+    all_but_one(r.got_two, 2).wait_recv()
+    every(0, GROUPS, slot_probs)
+    every(0, 4, slot_values)
 
     def slot_grads(group):
         got_scores = r.got_two[:, 48:64, :].reshape(SLOT_ROWS, 128)

time: 226 us -> 224 us (level)
  no operation moved by 1% of the time
where the time goes in v3:
time: 224 us
  Pallas kernels  223 us (100%)
    pallas_call x1, Pallas kernels, layer(): pl.pallas_call(partial(layer_kernel, names), out_shape=tuple((jax.ShapeDt...  216 us
    pallas_call x1, Pallas kernels, finish(): pl.pallas_call(partial(finish_kernel, count), out_shape=tuple((jax.ShapeD...  6.64 us

profile of v3, /device:TPU:0, one launch (start us, length us, event | category | flops | bytes accessed | tf_op | source)
XLA Modules:
  0.0 223.6 jit_solution(14699641798276093228)
XLA Ops:
  0.7 216.1 %layer.1 = (bf16[768,768]{1,0:T(8,128)(2,1)}, f32[1024,768]{1,0:T(8,128)}, f32[48,768]{1,0:T(8,128)}, f32[48,768]{1,0:T(8,128)}, f32[48,768]{1,0:T(8,128)}, /*in...) custom-call(bf16[1024,768]{1,0:T(8,128)(2,1)} %refs_0_.1, ...), custom_call_target="tpu_custom_call" | custom-call | tf_op jit(solution)/shard_map/layer/pallas_call | solution.py:1682
  216.8 6.6 %finish.1 = (bf16[768,768]{1,0:T(8,128)(2,1)}, f32[1024,768]{1,0:T(8,128)}, f32[48,768]{1,0:T(8,128)}, f32[48,768]{1,0:T(8,128)}, f32[48,768]{1,0:T(8,128)}, /*i...) custom-call(bf16[768,768]{1,0:T(8,128)(2,1)} %get-tuple-element.46.r, ...), custom_call_target="tpu_custom_call" | custom-call | tf_op jit(solution)/shard_map/finish/pallas_call | solution.py:1720

commit v4 on v3

--- a/solution.py
+++ b/solution.py
@@ -793,6 +793,7 @@
     )
     begin_a()
     begin_b()
+    begin_c()
 
     def move(*steps):
         for moves, first_step in steps:
@@ -865,15 +866,14 @@
         every(lax.div(quarter, 3), quarter_size, send)
         pl.when(quarter == 0)(partial(move, (moves_a, 0)))
         pl.when(quarter == 1)(partial(move, (moves_b, 0)))
-        pl.when(quarter == 2)(partial(move, (moves_a, 2)))
-        pl.when(quarter == 3)(partial(move, (moves_b, 2)))
+        pl.when(quarter == 2)(partial(move, (moves_c, 0)))
+        pl.when(quarter == 3)(partial(move, (moves_a, 2)))
 
     every(0, 4, quarter_rows)
-    begin_c()
     own_at = pl.ds(pl.multiple_of(me * PAD, 16), PAD)
     r.replies[:, own_at, :] = r.rows[:, own_at, :]
 
-    move((moves_a, 4))
+    move((moves_b, 2), (moves_c, 2))
 
     small_here = pl.ds(pl.multiple_of(chip * 128, 128), 128)
     lines = [r.bq, r.bv, r.bo, r.g1, r.s1, r.bdown, r.g2, r.s2]
@@ -895,7 +895,7 @@
         return remote(part, part, r.small_send.at[0], r.small_recv.at[0], 1 - core, chip)
 
     every(1, CHIPS, lambda step: small_copy(step).start())
-    move((moves_b, 4))
+    move((moves_a, 4))
 
     own_row = jnp.concatenate([r.ids[j : j + 1, :] for j in range(TOKENS // 128)], axis=1)
     owner_row = over(own_row, VOCAB_ROWS).astype(FULL)
@@ -906,7 +906,7 @@
     own_slot = own_group * SLOT_ROWS + owner_col * PAD + (own_rank - own_group * PAD)
     r.slot_col[...] = own_slot
     r.slot_line[0:1, :] = as_row(own_slot)
-    move((moves_a, 6), (moves_c, 0))
+    move((moves_b, 4), (moves_c, 4))
 
     at_sent = over(iota((1, TOKENS), 1), LONG)
     lens = jnp.concatenate(
@@ -952,7 +952,7 @@
     r.pairs_col[:, 0:1] = as_column(weight_line)
     r.pairs_col[:, 1:2] = as_column(pair_line.astype(FULL))
     r.pairs_col[:, 2:3] = as_column(side_line.astype(FULL))
-    move((moves_b, 6), (moves_c, 2))
+    move((moves_a, 6))
 
     all_smalls().wait_recv()
     smalls = r.smalls[...].astype(FULL)
@@ -975,7 +975,7 @@
     r.qkv_bias[0:1, WIDTH : 2 * WIDTH] = jnp.zeros((1, WIDTH), FULL)
     r.qkv_bias[0:1, 2 * WIDTH : 3 * WIDTH] = vector(1)
 
-    move((moves_a, 8), (moves_b, 8), (moves_c, 4))
+    move((moves_b, 6), (moves_c, 6))
 
     def first_row(source):
         code = jnp.where(r.rank[pl.ds(source, 1), :] >= 0.0, r.code[pl.ds(source, 1), :], 0.0)
@@ -1000,8 +1000,9 @@
         slot_at = iota((SLOT_ROWS, TOKENS), 0) + group * SLOT_ROWS
         named = (slot_at.astype(FULL) == r.slot_line[0:1, :]).astype(LOW)
         r.slot_hot[group] = named
-    moves_a[10]()
-    moves_b[10]()
+    move((moves_a, 8), (moves_b, 8), (moves_c, 8))
+    for moves in (moves_a, moves_b, moves_c):
+        moves[10]()
     finish_a()
     for quarter in range(4):
         rows_of(quarter).wait_recv()
@@ -1017,7 +1018,6 @@
         at = pl.ds(pl.multiple_of(tile * BLOCK, BLOCK), BLOCK)
         r.qkv[:, at] = (dot(r.embedded[...], r.wa[:, at]) + r.qkv_bias[0:1, at]).astype(LOW)
 
-    move((moves_c, 6))
     every(0, 9, project)
 
     row_sent = within(iota((PAIR_ROWS, WIDTH), 0), PAD)
@@ -1154,13 +1154,6 @@
     every(0, WIDE // WIDTH, up_part)
     steps_e[1]()
 
-    def attend_step(unit):
-        attend(unit)
-        pl.when(unit == 1)(partial(move, (moves_c, 8)))
-        pl.when(unit == 3)(moves_c[10])
-        pl.when(unit == 4)(steps_e[2])
-
-    every(0, 6, attend_step)
     finish_c()
 
     def pack_tall(target, first_row, act):
@@ -1243,23 +1236,18 @@
 
     r.got_one[me] = r.mail_one[me]
 
-    def open_step(tile):
-        open_tile(tile)
-        pl.when(tile == 0)(steps_e[3])
-        pl.when(tile == 2)(steps_u[4])
-
-    def feed_step(steps, part):
-        feed_up(part)
-        for index in range(6):
-            step = 6 * part + index + 1
-            pl.when(step < DEVICES)(partial(post_one, r.mail_one, r.got_one, 1, step))
-        for index, step in steps:
-            pl.when(part == index)(step)
-
-    first_parts, parts = 6, WIDE // BLOCK
-    every(0, TOKENS // BLOCK, open_step)
-    r.tile_up[...] = up_product(0)
-    every(0, first_parts, partial(feed_step, [(1, steps_u[5]), (2, steps_e[4]), (5, steps_e[5])]))
+    def attend_step(unit):
+        attend(unit)
+        for index in range(8):
+            step = 8 * (unit - 2) + index + 1
+            pl.when((step > 0) & (step < DEVICES))(
+                partial(post_one, r.mail_one, r.got_one, 1, step)
+            )
+        for index, step in [(0, steps_e[2]), (1, steps_u[4]), (3, steps_u[5]), (4, steps_e[3])]:
+            pl.when(unit == index)(step)
+
+    every(0, 6, attend_step)
+    steps_e[4]()
 
     units = r.units[...].reshape(SLOT_ROWS, WIDTH)
     weight_row, pair_row, side_row = r.pairs[0:1, :], r.pairs[1:2, :], r.pairs[2:3, :]
@@ -1421,18 +1409,18 @@
         r.active_turned[...] = jnp.transpose(gelu(up_pre)).astype(LOW)
         r.hidden_turned[...] = jnp.transpose(all_rows(r.early, 0))
 
-    rest = [steps_d[3], steps_a[3], steps_q[2], steps_d[4], steps_a[4]]
-    rest = [(first_parts + index, step) for index, step in enumerate(rest)]
-    every(first_parts, parts - 1, partial(feed_step, rest))
-    feed_up(parts - 1, last=True)
-
-    def rest_step(part):
-        feed_rest(part)
-        for index, step in enumerate([steps_q[3], steps_d[5], steps_a[5]]):
-            pl.when(part == index)(step)
-
-    every(0, WIDTH // BLOCK, rest_step)
-    steps_q[4]()
+    steps_e[5]()
+
+    def open_step(tile):
+        open_tile(tile)
+        pl.when(tile == 0)(steps_d[3])
+        pl.when(tile == 2)(steps_a[3])
+
+    def feed_step(part):
+        feed_up(part)
+        rest = [steps_q[2], steps_d[4], steps_a[4], steps_q[3], steps_d[5], steps_a[5], steps_q[4]]
+        for index, step in enumerate(rest):
+            pl.when(part == index + index // 5)(step)
 
     def down_step(part):
         feed_down(part)
@@ -1440,6 +1428,11 @@
             for end in ends:
                 pl.when(part == index)(end)
 
+    every(0, TOKENS // BLOCK, open_step)
+    r.tile_up[...] = up_product(0)
+    every(0, WIDE // BLOCK - 1, feed_step)
+    feed_up(WIDE // BLOCK - 1, last=True)
+    every(0, WIDTH // BLOCK, feed_rest)
     every(0, WIDTH // BLOCK, down_step)
     every(0, TOKENS // BLOCK, close_tile)
     every(0, 4, slot_queries)

time: 224 us -> 225 us (level)
  no operation moved by 1% of the time
where the time goes in v4:
time: 225 us
  Pallas kernels  224 us (100%)
    pallas_call x1, Pallas kernels, layer(): pl.pallas_call(partial(layer_kernel, names), out_shape=tuple((jax.ShapeDt...  217 us
    pallas_call x1, Pallas kernels, finish(): pl.pallas_call(partial(finish_kernel, count), out_shape=tuple((jax.ShapeD...  6.64 us

profile of v4, /device:TPU:0, one launch (start us, length us, event | category | flops | bytes accessed | tf_op | source)
XLA Modules:
  0.0 224.9 jit_solution(4127429250869855184)
XLA Ops:
  0.7 217.4 %layer.1 = (bf16[768,768]{1,0:T(8,128)(2,1)}, f32[1024,768]{1,0:T(8,128)}, f32[48,768]{1,0:T(8,128)}, f32[48,768]{1,0:T(8,128)}, f32[48,768]{1,0:T(8,128)}, /*in...) custom-call(bf16[1024,768]{1,0:T(8,128)(2,1)} %refs_0_.1, ...), custom_call_target="tpu_custom_call" | custom-call | tf_op jit(solution)/shard_map/layer/pallas_call | solution.py:1675
  218.1 6.6 %finish.1 = (bf16[768,768]{1,0:T(8,128)(2,1)}, f32[1024,768]{1,0:T(8,128)}, f32[48,768]{1,0:T(8,128)}, f32[48,768]{1,0:T(8,128)}, f32[48,768]{1,0:T(8,128)}, /*i...) custom-call(bf16[768,768]{1,0:T(8,128)(2,1)} %get-tuple-element.46.r, ...), custom_call_target="tpu_custom_call" | custom-call | tf_op jit(solution)/shard_map/finish/pallas_call | solution.py:1713

commit v5 on v3

--- a/solution.py
+++ b/solution.py
@@ -1196,11 +1196,10 @@
         return run
 
     def pack_coefs(coefs):
-        shape = (2 * PAIR_ROWS, GROUPS * 128)
-        row, lane = iota(shape, 0), iota(shape, 1)
-        kind = jnp.where(row >= PAIR_ROWS, PAD, 0)
-        head = over(row, PAD) - jnp.where(row >= PAIR_ROWS, HEADS, 0)
-        folds = head + kind + over(lane, 128) * 2 * PAD == within(lane, 128)
+        shape = (PAIR_ROWS, GROUPS * 128)
+        folds = over(iota(shape, 0), PAD) + over(iota(shape, 1), 128) * PAD == within(
+            iota(shape, 1), 128
+        )
         lanes = contract(coefs, folds.astype(LOW), 0, 0).astype(LOW)
         total = None
         for group in range(GROUPS):
@@ -1233,6 +1232,7 @@
         pl.when(part == 4)(steps_u[2])
 
     every(0, CHIPS // 2, pack_one_step)
+    r.mail_one[:, 64:80, :] = pack_coefs(probs_low)
     steps_u[3]()
 
     def post_one(box, got, index, step):
@@ -1333,7 +1333,7 @@
     inner = jnp.sum(probs * prob_grad, axis=1, keepdims=True)
     score_grad = (probs * (prob_grad - inner)).astype(LOW)
     steps_a[1]()
-    r.mail_two[:, 48:64, :] = pack_coefs(jnp.concatenate([probs_low, score_grad], axis=0))
+    r.mail_two[:, 48:64, :] = pack_coefs(score_grad)
     r.got_two[me, 48:64, :] = r.mail_two[me, 48:64, :]
     query_grad = (fold(dot(score_grad, r.qkv[:, keys])) * scale).astype(LOW)
     probs_total = jnp.sum(probs_low.astype(FULL), axis=1, keepdims=True)
@@ -1356,23 +1356,15 @@
 
     pack_two = pack_tall(r.mail_two, 0, with_sums)
 
-    def send_two(at):
-        remote(
-            r.mail_two.at[at],
-            r.got_two.at[me],
-            r.one_send.at[2],
-            r.one_recv.at[2],
-            lax.div(at, CHIPS),
-            lax.rem(at, CHIPS),
-        ).start()
-
     def pack_two_step(step):
         part = lax.rem(step + lax.div(me, 4), CHIPS // 2)
         pack_two(part)
         for index in range(4):
             turn = lax.rem(index + me, 4)
             at = lax.div(turn, 2) * CHIPS + 2 * part + lax.rem(turn, 2)
-            pl.when(at != me)(partial(send_two, at))
+            pl.when(at != me)(
+                partial(post_one, r.mail_two, r.got_two, 2, lax.rem(at + DEVICES - me, DEVICES))
+            )
 
     every(0, CHIPS // 2, pack_two_step)
     r.got_two[me, 0:48, :] = r.mail_two[me, 0:48, :]
@@ -1395,9 +1387,8 @@
         part = buffer[lax.div(quarter, 2), planes, :, :, start : start + BLOCK]
         return part.reshape(quarter_rows_count, BLOCK)
 
-    def widened(coefs, group, start, kind):
-        lane_head = over(iota((128, BLOCK), 1) + start, HEAD)
-        lanes = iota((128, BLOCK), 0) == lane_head + group * 2 * PAD + kind
+    def widened(coefs, group, start):
+        lanes = iota((128, BLOCK), 0) == over(iota((128, BLOCK), 1) + start, HEAD) + group * PAD
         return dot(coefs, lanes.astype(LOW))
 
     half_wide = WIDE // 2
@@ -1448,9 +1439,9 @@
 
     all_but_one(r.got_one, 1).wait_recv()
     def slot_probs(group):
-        got = r.got_two[:, 48:64, :].reshape(SLOT_ROWS, 128)
+        got_probs = r.got_one[:, 64:80, :].reshape(SLOT_ROWS, 128)
         for start in range(0, WIDTH, BLOCK):
-            r.replies[group, :, start : start + BLOCK] = widened(got, group, start, 0).astype(LOW)
+            r.replies[group, :, start : start + BLOCK] = widened(got_probs, group, start).astype(LOW)
 
     def slot_values(quarter):
         sents, span = from_sent(quarter)
@@ -1460,6 +1451,9 @@
             rows = rows.reshape(GROUPS, quarter_rows_count, BLOCK)
             rows = r.replies[:, span, lanes].astype(FULL) * rows
             r.replies[:, span, lanes] = rows.astype(LOW)
+
+    every(0, GROUPS, slot_probs)
+    every(0, 4, slot_values)
 
     def head_products(got, first_row, right, start, target):
         def one_head(head):
@@ -1516,15 +1510,13 @@
     for quarter in range(4):
         rows_of(quarter).wait_send()
     all_but_one(r.got_two, 2).wait_recv()
-    every(0, GROUPS, slot_probs)
-    every(0, 4, slot_values)
 
     def slot_grads(group):
         got_scores = r.got_two[:, 48:64, :].reshape(SLOT_ROWS, 128)
         for start in range(0, WIDTH, BLOCK):
             lanes = slice(start, start + BLOCK)
             rows = r.slot_query[group, :, lanes].astype(FULL)
-            rows = widened(got_scores, group, start, PAD) * rows * scale
+            rows = widened(got_scores, group, start) * rows * scale
             r.slot_query[group, :, lanes] = rows.astype(LOW)
         for start in range(0, WIDTH, BLOCK):
             lanes = slice(start, start + BLOCK)
@@ -1659,8 +1651,8 @@
         active_turned=pltpu.VMEM((2 * deep, SLOT_ROWS), LOW),
         left_turned=pltpu.VMEM((128, SLOT_ROWS), LOW),
         totals=pltpu.VMEM((8, WIDTH), FULL),
-        mail_one=pltpu.VMEM((DEVICES, 64, 128), LOW),
-        got_one=pltpu.VMEM((DEVICES, 64, 128), LOW),
+        mail_one=pltpu.VMEM((DEVICES, 80, 128), LOW),
+        got_one=pltpu.VMEM((DEVICES, 80, 128), LOW),
         mail_two=pltpu.VMEM((DEVICES, 64, 128), LOW),
         got_two=pltpu.VMEM((DEVICES, 64, 128), LOW),
         rows_send=dma((4,)),

time: 224 us -> 227 us (1.013)
    pallas_call x1, Pallas kernels: 216 us -> 219 us  [layer(): pl.pallas_call(partial(layer_kernel, names), out_shape=tuple((jax.ShapeDt...]
where the time goes in v5:
time: 227 us; the launch traced here: 226 us
  Pallas kernels  225 us (99%)
    pallas_call x1, Pallas kernels, layer(): pl.pallas_call(partial(layer_kernel, names), out_shape=tuple((jax.ShapeDt...  219 us
    pallas_call x1, Pallas kernels, finish(): pl.pallas_call(partial(finish_kernel, count), out_shape=tuple((jax.ShapeD...  6.64 us

profile of v5, /device:TPU:0, one launch (start us, length us, event | category | flops | bytes accessed | tf_op | source)
XLA Modules:
  0.0 226.1 jit_solution(15644135048775801321)
XLA Ops:
  0.7 218.6 %layer.1 = (bf16[768,768]{1,0:T(8,128)(2,1)}, f32[1024,768]{1,0:T(8,128)}, f32[48,768]{1,0:T(8,128)}, f32[48,768]{1,0:T(8,128)}, f32[48,768]{1,0:T(8,128)}, /*in...) custom-call(bf16[1024,768]{1,0:T(8,128)(2,1)} %refs_0_.1, ...), custom_call_target="tpu_custom_call" | custom-call | tf_op jit(solution)/shard_map/layer/pallas_call | solution.py:1674
  219.3 6.6 %finish.1 = (bf16[768,768]{1,0:T(8,128)(2,1)}, f32[1024,768]{1,0:T(8,128)}, f32[48,768]{1,0:T(8,128)}, f32[48,768]{1,0:T(8,128)}, f32[48,768]{1,0:T(8,128)}, /*i...) custom-call(bf16[768,768]{1,0:T(8,128)(2,1)} %get-tuple-element.46.r, ...), custom_call_target="tpu_custom_call" | custom-call | tf_op jit(solution)/shard_map/finish/pallas_call | solution.py:1712

commit v6 on v0

--- a/solution.py
+++ b/solution.py
@@ -1255,16 +1255,16 @@
 
     def feed_step(steps, part):
         feed_up(part)
-        for index in range(3):
-            step = 3 * part + index + 1
+        for index in range(4):
+            step = 4 * part + index + 1
             pl.when(step < DEVICES)(partial(post_one, r.mail_one, r.got_one, 1, step))
         for index, step in steps:
             pl.when(part == index)(step)
 
-    first_parts, parts = 6, WIDE // BLOCK
+    first_parts, parts = 4, WIDE // BLOCK
     every(0, TOKENS // BLOCK, open_step)
     r.tile_up[...] = up_product(0)
-    every(0, first_parts, partial(feed_step, [(1, steps_u[5]), (2, steps_e[4]), (5, steps_e[5])]))
+    every(0, first_parts, partial(feed_step, [(1, steps_u[5]), (2, steps_e[4]), (3, steps_e[5])]))
 
     units = r.units[...].reshape(SLOT_ROWS, WIDTH)
     weight_row, pair_row, side_row = r.pairs[0:1, :], r.pairs[1:2, :], r.pairs[2:3, :]

time: 221 us -> 224 us (1.014)
  Pallas kernels: 220 us -> 223 us
    pallas_call x1, Pallas kernels: 213 us -> 216 us  [layer(): pl.pallas_call(partial(layer_kernel, names), out_shape=tuple((jax.ShapeDt...]
where the time goes in v6:
time: 224 us
  Pallas kernels  223 us (100%)
    pallas_call x1, Pallas kernels, layer(): pl.pallas_call(partial(layer_kernel, names), out_shape=tuple((jax.ShapeDt...  216 us
    pallas_call x1, Pallas kernels, finish(): pl.pallas_call(partial(finish_kernel, count), out_shape=tuple((jax.ShapeD...  6.64 us

profile of v6, /device:TPU:0, one launch (start us, length us, event | category | flops | bytes accessed | tf_op | source)
XLA Modules:
  0.0 223.8 jit_solution(7912272073596144436)
XLA Ops:
  0.7 216.4 %layer.1 = (bf16[768,768]{1,0:T(8,128)(2,1)}, f32[1024,768]{1,0:T(8,128)}, f32[48,768]{1,0:T(8,128)}, f32[48,768]{1,0:T(8,128)}, f32[48,768]{1,0:T(8,128)}, /*in...) custom-call(bf16[1024,768]{1,0:T(8,128)(2,1)} %refs_0_.1, ...), custom_call_target="tpu_custom_call" | custom-call | tf_op jit(solution)/shard_map/layer/pallas_call | solution.py:1663
  217.0 6.6 %finish.1 = (bf16[768,768]{1,0:T(8,128)(2,1)}, f32[1024,768]{1,0:T(8,128)}, f32[48,768]{1,0:T(8,128)}, f32[48,768]{1,0:T(8,128)}, f32[48,768]{1,0:T(8,128)}, /*i...) custom-call(bf16[768,768]{1,0:T(8,128)(2,1)} %get-tuple-element.46.r, ...), custom_call_target="tpu_custom_call" | custom-call | tf_op jit(solution)/shard_map/finish/pallas_call | solution.py:1701
